TPU v7x, 32 devices: a whole 2x2x4 slice. The times are simulated.
32 devices in a mesh: groups: 2 (over y), sec: 4 (over z), term: 4 (over x, core).
Axes of the slice: x: 2, y: 2, z: 4, core: 2. Of those that a mesh axis runs over, the one named last changes fastest.
Arguments:
- psi: bfloat16 [64, 2, 16, 128, 128], P(('groups', 'sec')), parts along dimension 0, may hold values from -6 to 6
- left_env: bfloat16 [64, 16, 128, 128], P(('groups', 'sec'), 'term'), parts along dimension 0
- right_env: bfloat16 [64, 16, 128, 128], P(('groups', 'sec'), 'term'), parts along dimension 0
- local_ops: bfloat16 [8, 16, 16], replicated
- term_op: int32 [16], P('term'), may hold values from 0 to 7
- sector_rows: int32 [64], P('groups'), parts along dimension 0, may hold values from 64 to 128, as said below
- block_partner: int32 [64, 2], P(('groups', 'sec')), parts along dimension 0, may hold values from 0 to 31, as said below
- block_count: int32 [64], P(('groups', 'sec')), parts along dimension 0, may hold values from 1 to 2, as said below
Outputs:
- residual: bfloat16 [64, 2, 16, 128, 128], P(('groups', 'sec')), parts along dimension 0
- rayleigh: float32 [2], P('groups'), parts along dimension 0
There are 2 independent parts, one for each index of `groups`. A program takes and returns all parts, laid end to end along the dimension named above; an argument that names none is the same for every part. Nothing has to cross between parts.
Inputs may be any that keep to these rules, and one draw needn't show every extreme that they name: `sector_rows`: some sector has all 128 rows live. `block_partner`: the 2 partner sectors of one left sector are distinct. `block_count`: some sector has all 2 blocks live.
All inputs are finite; a program needn't handle non-finite values.
Results may differ from a plain program's by a relative error of at most 0.0045.
Values may be sent and summed in bfloat16 or wider, within the bound.
No kernel may reach another device: no remote copies, remote signals or barrier semaphores. Data moves between devices by JAX's collectives and lax.ppermute only.
A program may use at most 192 MiB of HBM per device.

v0:
```python
import functools

import jax
import jax.numpy as jnp
from jax import lax
from jax.experimental import pallas as pl
from jax.experimental.pallas import tpu as pltpu
from jax.sharding import PartitionSpec as P

TILE = 16
WIDE = 2
MIB = 1024 * 1024
SPARE = 3 * MIB // 2
HASTE = 256


def block_facts(scalars, index, slot):
    meta, places, sector_rows, partners, counts = scalars
    sector = places[index]
    live = slot < counts[sector]
    own_rows = sector_rows[meta[0] + sector]
    partner_rows = sector_rows[partners[sector, slot]]
    return sector, live, own_rows, partner_rows


def live_entries(own_rows, partner_rows, width):
    left = lax.broadcasted_iota(jnp.int32, (1, width, width), 1) < own_rows
    right = lax.broadcasted_iota(jnp.int32, (1, width, width), 2) < partner_rows
    return left & right


def folded(values):
    states, width = values.shape[0], values.shape[-1]
    return jnp.sum(values.reshape(states * width // 8, 8, width), axis=0)


def by_live_rows(own_rows, groups, work):
    few = 3 * groups // 4
    pl.when(own_rows <= few * TILE)(functools.partial(work, few))
    pl.when(own_rows > few * TILE)(functools.partial(work, groups))


def spread_operators(ops_ref, chosen, spread_ops, at, states):
    width, wide = ops_ref.shape[-1], states * TILE
    row_state = lax.broadcasted_iota(jnp.int32, (wide, states), 0) // TILE
    column = lax.broadcasted_iota(jnp.int32, (wide, states), 1)
    pick_rows = (row_state == column).astype(jnp.bfloat16)
    row = lax.broadcasted_iota(jnp.int32, (width, wide), 0)
    column_state = lax.broadcasted_iota(jnp.int32, (width, wide), 1) // TILE
    pick_columns = (row == column_state).astype(jnp.bfloat16)
    inner_row = lax.rem(lax.broadcasted_iota(jnp.int32, (wide, wide), 0), TILE)
    inner_column = lax.rem(lax.broadcasted_iota(jnp.int32, (wide, wide), 1), TILE)
    for term in chosen:
        operator = ops_ref[term * states : (term + 1) * states, :]
        rows = jnp.dot(pick_rows, operator, preferred_element_type=jnp.float32)
        full = jnp.dot(
            rows.astype(jnp.bfloat16), pick_columns, preferred_element_type=jnp.float32
        )
        spread_ops[at] = jnp.where(inner_row == inner_column, full, 0.0).astype(jnp.bfloat16)
        at += 1


def multiply_left(groups, lefts, live_psi, after_left):
    rows = groups * TILE
    states, width = live_psi.shape[0], live_psi.shape[-1]
    stacked = jnp.concatenate(lefts, axis=0)
    for pair in range(states // WIDE):
        columns = jnp.concatenate([live_psi[pair * WIDE + at] for at in range(WIDE)], axis=1)
        done = jnp.dot(stacked, columns, preferred_element_type=jnp.float32).astype(jnp.bfloat16)
        for term in range(len(lefts)):
            for at in range(WIDE):
                state = pair * WIDE + at
                after_left[term, :groups, state * TILE : (state + 1) * TILE, :] = done[
                    term * rows : (term + 1) * rows, at * width : (at + 1) * width
                ].reshape(groups, TILE, width)


def apply_operators(low, high, spread_ops, after_left, targets):
    width = after_left.shape[-1]
    for group in range(low, high, WIDE):
        for term, (target, lead) in enumerate(targets):
            columns = jnp.concatenate(
                [after_left[term, group + at] for at in range(WIDE)], axis=1
            )
            done = jnp.dot(
                spread_ops[term], columns, preferred_element_type=jnp.float32
            ).astype(jnp.bfloat16)
            for at in range(WIDE):
                target[(*lead, group + at)] = done[:, at * width : (at + 1) * width]


def each_live_block(half, slots, scalars, work):
    meta = scalars[0]

    def visit(block, carry):
        place, slot = block // slots, lax.rem(block, slots)
        sector, live, own_rows, partner_rows = block_facts(
            scalars, meta[1] * half + place, slot
        )
        pl.when(live)(functools.partial(work, block, place, sector, own_rows, partner_rows))
        return carry

    lax.fori_loop(0, half * slots, visit, 0)


def pack_kernel(chunks, half, terms, places, term_op, ops_ref, left_ref, right_ref, *rest):
    payloads, rest = rest[:2], rest[2:]
    shares, sems = rest[: len(chunks)], rest[len(chunks)]
    states, width = ops_ref.shape[1], left_ref.shape[-1]
    copied = half * terms * width
    for part, payload in enumerate(payloads):
        for place in range(half):
            pltpu.make_async_copy(
                left_ref.at[places[part * half + place]],
                payload.at[pl.ds(place * terms * width, terms * width)],
                sems.at[part],
            ).start()
    moves = []
    for at, (start, length) in enumerate(chunks):
        move = pltpu.make_async_copy(
            right_ref.at[:, pl.ds(start, length)], shares[at], sems.at[2 + at]
        )
        move.start()
        moves.append(move)
    for payload in payloads:
        for term in range(terms):
            rows = slice(copied + term * states, copied + (term + 1) * states)
            payload[rows, :] = jnp.zeros((states, width), jnp.bfloat16)
            payload[rows, :states] = ops_ref[term_op[term]]
    for part, payload in enumerate(payloads):
        whole = payload.at[pl.ds(0, copied)]
        pltpu.make_async_copy(whole, whole, sems.at[part]).wait()
    for move in moves:
        move.wait()


def pack_call(chunks, places, term_op, local_ops, left_env, right_env):
    sectors, terms, width = left_env.shape[:3]
    half, states = sectors // 2, local_ops.shape[1]
    payload = jax.ShapeDtypeStruct((terms * (half * width + states), width), jnp.bfloat16)
    shares = [
        jax.ShapeDtypeStruct((sectors, length, width, width), jnp.bfloat16)
        for start, length in chunks
    ]
    return pl.pallas_call(
        functools.partial(pack_kernel, chunks, half, terms),
        in_specs=in_smem(2) + resident(1) + [pl.BlockSpec(memory_space=pltpu.HBM)] * 2,
        out_specs=resident(2 + len(chunks)),
        out_shape=[payload, payload] + shares,
        scratch_shapes=[pltpu.SemaphoreType.DMA((2 + len(chunks),))],
        compiler_params=pltpu.CompilerParams(vmem_limit_bytes=58 * MIB),
        cost_estimate=pl.CostEstimate(
            flops=0, bytes_accessed=4 * left_env.size, transcendentals=0
        ),
        name="pack",
    )(places, term_op, local_ops, left_env.reshape(sectors, terms * width, width), right_env)


def source_views(payloads):
    views = []
    for payload in payloads:
        views += [payload] if len(payload.shape) == 2 else [payload.at[0], payload.at[1]]
    return views


def term_rows(view, place, held, term, rows):
    width = view.shape[-1]
    return view[pl.ds(pl.multiple_of((place * held + term) * width, width), rows), :]


def left_kernel(first, held, items, count, afters, half, slots, meta, places, sector_rows,
                partners, counts, *rest):
    scalars = (meta, places, sector_rows, partners, counts)
    psi_ref, rest = rest[afters], rest[afters + 1 :]
    payloads, rest = rest[:count], rest[count:]
    outs, rest = rest[: len(items)], rest[len(items) :]
    token_ref, rest = rest[0], rest[1:]
    if first:
        live_psi, square_ref, spread_ops, after_left, sems = rest
    else:
        live_psi = psi_ref
        spread_ops, after_left = rest
    states, width = live_psi.shape[1], live_psi.shape[-1]
    views = source_views(payloads)

    def fetch(block, sector):
        return pltpu.make_async_copy(
            psi_ref.at[sector, lax.rem(block, slots)], live_psi.at[block], sems.at[block]
        )

    if first:
        each_live_block(
            half, slots, scalars, lambda block, place, sector, *rows: fetch(block, sector).start()
        )
        square_ref[...] = jnp.zeros_like(square_ref)
    at = 0
    for source, start, terms in items:
        operators = views[source][half * held * width :, :]
        spread_operators(operators, range(start, start + terms), spread_ops, at, states)
        at += terms
    token_ref[...] = jnp.zeros_like(token_ref)

    def work(block, place, sector, own_rows, partner_rows):
        if first:
            fetch(block, sector).wait()
            mask = live_entries(own_rows, partner_rows, width)
            kept = jnp.where(mask, live_psi[block], jnp.zeros((), jnp.bfloat16))
            live_psi[block] = kept
            wide_psi = kept.astype(jnp.float32)
            square_ref[...] += folded(wide_psi * wide_psi)
        targets = [
            (outs[at], (block, term))
            for at, (source, start, terms) in enumerate(items)
            for term in range(terms)
        ]

        def multiply(groups):
            lefts = [
                term_rows(views[source], place, held, start + term, groups * TILE)
                for source, start, terms in items
                for term in range(terms)
            ]
            multiply_left(groups, lefts, live_psi.at[block], after_left)
            apply_operators(0, groups, spread_ops, after_left, targets)

        by_live_rows(own_rows, width // TILE, multiply)

    each_live_block(half, slots, scalars, work)


def resident(count):
    return [pl.BlockSpec(memory_space=pltpu.VMEM)] * count


def in_smem(count):
    return [pl.BlockSpec(memory_space=pltpu.SMEM)] * count


def left_call(first, scalars, held, items, shape, psi, payloads, afters):
    blocks, slots, states, width = shape
    groups, wide = width // TILE, states * TILE
    every = sum(terms for source, start, terms in items)
    fold_shape = jax.ShapeDtypeStruct((8, width), jnp.float32)
    out_shape = [
        jax.ShapeDtypeStruct((blocks, terms, groups, wide, width), jnp.bfloat16)
        for source, start, terms in items
    ] + [fold_shape]
    scratch = [
        pltpu.VMEM((every, wide, wide), jnp.bfloat16),
        pltpu.VMEM((every, groups, wide, width), jnp.bfloat16),
    ]
    if first:
        live_psi = jax.ShapeDtypeStruct((blocks, states, width, width), jnp.bfloat16)
        out_shape += [live_psi, fold_shape]
        scratch.append(pltpu.SemaphoreType.DMA((blocks,)))
    psi_spec = [pl.BlockSpec(memory_space=pltpu.HBM)] if first else resident(1)
    return pl.pallas_call(
        functools.partial(
            left_kernel, first, held, items, len(payloads), len(afters), blocks // slots, slots
        ),
        in_specs=in_smem(len(scalars))
        + [pl.BlockSpec(memory_space=pl.ANY)] * len(afters)
        + psi_spec
        + resident(len(payloads)),
        out_specs=resident(len(out_shape)),
        out_shape=out_shape,
        scratch_shapes=scratch,
        compiler_params=pltpu.CompilerParams(
            vmem_limit_bytes=max(
                28 * MIB if first else 0,
                SPARE + 2 * every * (wide * wide + groups * wide * width),
            )
        ),
        cost_estimate=pl.CostEstimate(
            flops=psi.size * every * (width + wide) // HASTE,
            bytes_accessed=psi.size // HASTE,
            transcendentals=0,
        ),
        name="left",
    )(*scalars, *afters, psi, *payloads)


def stack_kernel(start, near_ref, received_ref, both_ref):
    terms = both_ref.shape[2] if len(both_ref.shape) == 5 else None
    for side, ref in enumerate((near_ref, received_ref)):
        both_ref[side] = ref[...] if start is None else ref[:, start : start + terms]


def stack_call(near, received, chunk=None):
    start, terms = chunk or (None, None)
    shape = near.shape if chunk is None else (near.shape[0], terms) + near.shape[2:]
    return pl.pallas_call(
        functools.partial(stack_kernel, start),
        in_specs=resident(2),
        out_specs=resident(1)[0],
        out_shape=jax.ShapeDtypeStruct((2,) + shape, near.dtype),
        compiler_params=pltpu.CompilerParams(vmem_limit_bytes=SPARE),
        cost_estimate=pl.CostEstimate(flops=0, bytes_accessed=4096, transcendentals=0),
        name="stack",
    )(near, received)


def choose_kernel(line, count, afters, half, slots, meta, places, partners, *rest):
    rest = rest[afters:]
    pieces, (mine_ref, other_ref) = rest[:count], rest[count:]
    sectors = pieces[0].shape[1]
    for part, out_ref in enumerate((mine_ref, other_ref)):
        for block in range(half * slots):
            sector = places[(meta[1] ^ part) * half + block // slots]
            partner = partners[sector, block % slots]
            away = meta[3] ^ (partner // sectors)
            piece, side = away // 2, away & 1
            if line:
                inner = ((meta[3] + 1) & 2) // 2
                side = side ^ (piece & inner)
                piece = piece + (piece & (1 - inner))
            place = lax.rem(partner, sectors)
            for at in range(count):
                @pl.when(piece == at)
                def _(at=at, side=side, place=place, block=block, out_ref=out_ref):
                    out_ref[block] = pieces[at][side, place]


def choose_call(line, scalars, half, slots, pieces, afters):
    meta, places, _, partners, _ = scalars
    terms, width = pieces[0].shape[2:4]
    chosen = jax.ShapeDtypeStruct((half * slots, terms, width, width), jnp.bfloat16)
    return pl.pallas_call(
        functools.partial(choose_kernel, line, len(pieces), len(afters), half, slots),
        in_specs=in_smem(3)
        + [pl.BlockSpec(memory_space=pl.ANY)] * len(afters)
        + resident(len(pieces)),
        out_specs=resident(2),
        out_shape=[chosen, chosen],
        compiler_params=pltpu.CompilerParams(vmem_limit_bytes=SPARE),
        cost_estimate=pl.CostEstimate(flops=0, bytes_accessed=4096, transcendentals=0),
        name="choose",
    )(meta, places, partners, *afters, *pieces)


def chunk_kernel(first, last, held, chunk, ahead, late, count, half, slots,
                 meta, places, sector_rows, partners, counts, after_ref, psi_ref, *rest):
    start, terms = chunk
    early_refs, rest = rest[: len(ahead)], rest[len(ahead) :]
    payloads, rest = rest[:count], rest[count:]
    near_rights, rest = rest[:2], rest[2:]
    devices = len(ahead) + len(late)
    far_rights, rest = rest[: devices // 2 - 1], rest[devices // 2 - 1 :]
    if not first:
        sum_in, rest = rest[0], rest[1:]
    sum_out, fold_ref, *rest = rest
    if late:
        spread_ops, after_left, after_ops, *rest = rest
    states, width = psi_ref.shape[1], psi_ref.shape[-1]
    groups = width // TILE
    views = dict(zip(late, source_views(payloads)))
    rights = list(near_rights) + [right.at[side] for right in far_rights for side in (0, 1)]
    for at, source in enumerate(late):
        operators = views[source][half * held * width :, :]
        spread_operators(operators, range(start, start + terms), spread_ops, at * terms, states)
    fold_ref[...] = jnp.zeros_like(fold_ref)
    if last:
        sum_out[...] = jnp.zeros_like(sum_out)

    def work(block, place, sector, own_rows, partner_rows):
        total = rest[0] if last else sum_out.at[block]
        columns = [
            jnp.concatenate(
                [rights[pair + at][block, term] for at in range(2) for term in range(terms)],
                axis=0,
            )
            for pair in range(0, devices, 2)
        ]

        def operated(device, term, group):
            if device in ahead:
                return early_refs[ahead.index(device)][block, term, group]
            return after_ops[late.index(device) * terms + term, group]

        def multiply(live_groups):
            if late:
                lefts = [
                    term_rows(views[source], place, held, start + term, live_groups * TILE)
                    for source in late
                    for term in range(terms)
                ]
                multiply_left(live_groups, lefts, psi_ref.at[block], after_left)
            targets = [(after_ops, (term,)) for term in range(len(late) * terms)]
            for group in range(0, live_groups, WIDE):
                if late:
                    apply_operators(group, group + WIDE, spread_ops, after_left, targets)
                parts = []
                for pair in range(0, devices, 2):
                    rows = jnp.concatenate(
                        [
                            jnp.concatenate(
                                [
                                    operated(pair + at, term, group + side)
                                    for at in range(2)
                                    for term in range(terms)
                                ],
                                axis=1,
                            )
                            for side in range(WIDE)
                        ],
                        axis=0,
                    )
                    parts.append(
                        jnp.dot(rows, columns[pair // 2], preferred_element_type=jnp.float32)
                    )
                while len(parts) > 1:
                    parts = [parts[at] + parts[at + 1] for at in range(0, len(parts), 2)]
                done = parts[0].reshape(WIDE, states, TILE, width)
                for side in range(WIDE):
                    tile = slice((group + side) * TILE, (group + side + 1) * TILE)
                    if first:
                        total[:, tile, :] = done[side]
                    else:
                        total[:, tile, :] = sum_in[block, :, tile, :] + done[side]

        by_live_rows(own_rows, groups, multiply)
        if last:
            mask = live_entries(own_rows, partner_rows, width)
            kept = jnp.where(mask, total[...], 0.0)
            fold_ref[...] += folded(kept * psi_ref[block].astype(jnp.float32))
            sum_out[block] = kept.astype(jnp.bfloat16)

    each_live_block(half, slots, (meta, places, sector_rows, partners, counts), work)


def chunk_call(first, last, held, chunk, ahead, late, scalars, slots, psi, early, payloads,
               rights, total, after):
    blocks, states, width = psi.shape[:3]
    groups, wide = width // TILE, states * TILE
    start, terms = chunk
    operands = [after, psi, *early, *payloads, *rights]
    aliases = {}
    if not first:
        operands.append(total)
        if not last:
            aliases = {len(scalars) + len(operands) - 1: 0}
    sum_dtype = jnp.bfloat16 if last else jnp.float32
    every = len(late) * terms
    scratch = []
    if late:
        scratch += [
            pltpu.VMEM((every, wide, wide), jnp.bfloat16),
            pltpu.VMEM((every, groups, wide, width), jnp.bfloat16),
            pltpu.VMEM((every, groups, wide, width), jnp.bfloat16),
        ]
    if last:
        scratch.append(pltpu.VMEM((states, width, width), jnp.float32))
    work = psi.size * terms * ((len(ahead) + len(late)) * width + len(late) * (width + wide))
    return pl.pallas_call(
        functools.partial(
            chunk_kernel, first, last, held, chunk, ahead, late, len(payloads),
            blocks // slots, slots,
        ),
        in_specs=in_smem(len(scalars))
        + [pl.BlockSpec(memory_space=pl.ANY)]
        + resident(len(operands) - 1),
        out_specs=resident(2),
        out_shape=[
            jax.ShapeDtypeStruct(psi.shape, sum_dtype),
            jax.ShapeDtypeStruct((8, width), jnp.float32),
        ],
        scratch_shapes=scratch,
        input_output_aliases=aliases,
        compiler_params=pltpu.CompilerParams(
            vmem_limit_bytes=(len(ahead) + len(late)) * SPARE // 4
            + 2 * every * wide * (wide + 2 * groups * width)
            + 4 * int(last) * states * width * width
        ),
        cost_estimate=pl.CostEstimate(
            flops=work // HASTE, bytes_accessed=psi.size // HASTE, transcendentals=0
        ),
        name="chunk",
    )(*scalars, *operands)


def residual_kernel(half, slots, meta, places, sector_rows, partners, counts,
                    folds_ref, live_psi, own_ref, other_ref, psi_ref, out_ref, quotient_ref,
                    other_psi, staged, read_sems, write_sems):
    scalars = (meta, places, sector_rows, partners, counts)
    blocks, width = own_ref.shape[0], own_ref.shape[-1]
    depth = staged.shape[0]

    def where(block, side):
        index = (meta[1] ^ side) * half + block // slots
        return places[index], block % slots, index

    def read(block):
        sector, slot, _ = where(block, 1)
        return pltpu.make_async_copy(
            psi_ref.at[sector, slot], other_psi.at[block], read_sems.at[block]
        )

    def write(step):
        sector, slot, _ = where(step % blocks, step // blocks)
        return pltpu.make_async_copy(
            staged.at[step % depth], out_ref.at[sector, slot], write_sems.at[step % depth]
        )

    for block in range(blocks):
        read(block).start()
    quotient = jnp.sum(folds_ref[0:8, :]) / jnp.sum(folds_ref[8:16, :])
    quotient_ref[0] = quotient
    for step in range(2 * blocks):
        block, side = step % blocks, step // blocks
        if step >= depth:
            write(step - depth).wait()
        sector, slot, index = where(block, side)
        _, live, own_rows, partner_rows = block_facts(scalars, index, slot)
        mask = live_entries(jnp.where(live, own_rows, 0), partner_rows, width)
        if side:
            read(block).wait()
            values, sums = other_psi[block], other_ref[block]
        else:
            values, sums = live_psi[block], own_ref[block]
        scaled = quotient * jnp.where(mask, values.astype(jnp.float32), 0.0)
        staged[step % depth] = (sums.astype(jnp.float32) - scaled).astype(jnp.bfloat16)
        write(step).start()
    for step in range(2 * blocks - min(depth, 2 * blocks), 2 * blocks):
        write(step).wait()


def residual_call(scalars, folds, psi, live_psi, own, other):
    sectors, slots, states, width = psi.shape[:4]
    blocks = own.shape[0]
    depth = 4
    in_hbm = [pl.BlockSpec(memory_space=pltpu.HBM)]
    return pl.pallas_call(
        functools.partial(residual_kernel, sectors // 2, slots),
        in_specs=in_smem(len(scalars)) + resident(4) + in_hbm,
        out_specs=in_hbm + in_smem(1),
        out_shape=[
            jax.ShapeDtypeStruct(psi.shape, jnp.bfloat16),
            jax.ShapeDtypeStruct((1,), jnp.float32),
        ],
        scratch_shapes=[
            pltpu.VMEM((blocks, states, width, width), jnp.bfloat16),
            pltpu.VMEM((depth, states, width, width), jnp.bfloat16),
            pltpu.SemaphoreType.DMA((blocks,)),
            pltpu.SemaphoreType.DMA((depth,)),
        ],
        compiler_params=pltpu.CompilerParams(vmem_limit_bytes=41 * MIB),
        cost_estimate=pl.CostEstimate(
            flops=3 * psi.size, bytes_accessed=6 * psi.size, transcendentals=0
        ),
        name="residual",
    )(*scalars, folds, live_psi, own, other, psi)


def on_device(
    devices, rings, psi, left_env, right_env, local_ops, term_op, sector_rows, block_partner,
    block_count,
):
    sectors, slots, states, width = psi.shape[:4]
    terms = left_env.shape[1]
    half = sectors // 2
    me = lax.axis_index("term")
    ring = lax.axis_index("sec")
    core = me % 2
    meta = jnp.stack([ring * sectors, core, me, ring]).astype(jnp.int32)

    near_rows = lax.dynamic_slice_in_dim(sector_rows, ring * sectors, sectors)
    weight = block_count * (near_rows + width // 2)
    order = jnp.arange(sectors, dtype=jnp.int32)
    ahead = (weight[None, :] > weight[:, None]) | (
        (weight[None, :] == weight[:, None]) & (order[None, :] < order[:, None])
    )
    rank = jnp.sum(ahead.astype(jnp.int32), axis=1)
    index = ((rank ^ (rank >> 1)) & 1) * half + (rank >> 1)
    places = jnp.sum(jnp.where(index[None, :] == order[:, None], order[None, :], 0), axis=1)
    scalars = (meta, places, sector_rows, block_partner, block_count)

    def swap(value, bits, axis="term", size=devices):
        return lax.ppermute(value, axis, [(i, i ^ bits) for i in range(size)])

    def to_far_chips(near, received):
        both = stack_call(near, received)
        return both, [swap(both, bits) for bits in range(2, devices, 2)]

    chunks = [(at, 1) for at in range(terms)]
    ordered = jnp.roll(places, -core * half)
    parcels = [chunks[0], (chunks[0][1], terms - chunks[0][1])]
    mine, theirs, *shares = pack_call(
        parcels, ordered, term_op, local_ops, left_env, right_env
    )
    near_left = swap(theirs, 1)
    both_lefts, far_lefts = to_far_chips(mine, near_left)

    shards, rights = [], []
    swapped = [swap(share, 1, "sec", rings) for share in shares]
    line = rings == 4

    def gather():
        at = len(shards)
        if at == 0:
            pair = stack_call(shares[0], swapped[0])
        else:
            start, length = chunks[at]
            pair = stack_call(shares[1], swapped[1], (start - parcels[1][0], length))
        pieces = [pair]
        if line:
            pieces.append(lax.ppermute(pair, "sec", [(1, 2), (2, 1)]))
        bits = 2
        while bits < rings and not line:
            pieces = pieces + [swap(piece, bits, "sec", rings) for piece in pieces]
            bits *= 2
        shards.append(pieces)

    def choose(token):
        at = len(rights)
        afters = [token] + (rights[-1][2:] if rights else far_lefts)
        if 0 < at < len(chunks) - 1:
            afters.append(shards[at + 1][-1])
        pieces = shards[at]
        if line:
            pieces = pieces + [lax.ppermute(pieces[-1], "sec", [(1, 0), (2, 3)])]
        mine, other = choose_call(line, scalars, half, slots, pieces, afters)
        received = swap(other, 1)
        if at < len(chunks) - 1:
            both, far_rights = to_far_chips(mine, received)
        else:
            both = mine
            far_rights = [
                stack_call(swap(mine, bits), swap(other, bits + 1))
                for bits in range(2, devices, 2)
            ]
        rights.append([mine, received] + far_rights)
        return both

    products = {}
    shape = (half * slots, slots, states, width)
    far = tuple(range(2, devices))

    def go_left(sources, which, token, first=False, waits=()):
        items = [(source, *chunks[at]) for at in which for source in sources]
        near = [source for source in sources if source < 2]
        payloads = [(mine, near_left)[source] for source in near]
        if len(near) < len(sources):
            payloads += far_lefts
        renamed = [(sources.index(source), start, count) for source, start, count in items]
        outs = left_call(
            first, scalars, terms, renamed, shape, psi if first else live_psi, payloads,
            [token, *waits],
        )
        for at, out in zip([(at, source) for at in which for source in sources], outs):
            products[at] = out
        return outs[len(items) :]

    every = range(len(chunks))
    gather()
    token, live_psi, squares = go_left((0,), every, both_lefts, True)
    shards[0][-1], shares[1], swapped[1], _ = lax.optimization_barrier(
        (shards[0][-1], shares[1], swapped[1], token)
    )
    for chunk in chunks[1:]:
        gather()
    token, = go_left((1,), every[1:], token)
    token = choose(token)
    total = None
    for at, chunk in enumerate(chunks):
        last = at == len(chunks) - 1
        if len(rights) < len(chunks):
            token = choose(token)
        ahead = tuple(source for source in range(devices) if (at, source) in products)
        late = tuple(source for source in range(devices) if source not in ahead)
        payloads = ([near_left] if 1 in late else []) + (far_lefts if late else [])
        total, token = chunk_call(
            at == 0, last, terms, chunk, ahead, late, scalars, slots, live_psi,
            [products.pop((at, source)) for source in ahead], payloads,
            rights[at], total, token,
        )
        if at == len(chunks) - 3:
            token, = go_left(far, [len(chunks) - 1], token)

    other = swap(total, 1)
    folds = jnp.concatenate([token, squares], axis=0)
    parts = [folds] + [swap(folds, bits, "sec", rings) for bits in range(1, rings)]
    while len(parts) > 1:
        parts = [parts[at] + parts[at + 1] for at in range(0, len(parts), 2)]
    folds = parts[0]
    folds = folds + swap(folds, 1)
    residual, rayleigh = residual_call(scalars, folds, psi, live_psi, total, other)
    return residual, rayleigh


def solution(mesh):
    placed = (
        P(("groups", "sec"), None, None, None, None),
        P(("groups", "sec"), "term", None, None),
        P(("groups", "sec"), "term", None, None),
        P(),
        P("term"),
        P("groups"),
        P(("groups", "sec"), None),
        P(("groups", "sec")),
    )
    return jax.shard_map(
        functools.partial(on_device, mesh.shape["term"], mesh.shape["sec"]),
        mesh=mesh,
        in_specs=placed,
        out_specs=(P(("groups", "sec"), None, None, None, None), P("groups")),
        check_vma=False,
    )
```

profile of v0, /device:TPU:5, one launch (start us, length us, event | category | flops | bytes accessed | tf_op | source)
XLA Modules:
  0.0 154.5 jit_solution(7587507360271848614)
XLA Ops:
  2.5 3.8 %pack.1 = (bf16[2112,128]{1,0:T(8,128)(2,1)}, bf16[2112,128]{1,0:T(8,128)(2,1)}, bf16[8,1,128,128]{3,2,1,0:T(8,128)(2,1)}, bf16[8,3,128,128]{3,2,1,0:T(8,128)(2,1)}) custom-call(s32[8]{0:T(128)} %dynamic_slice.8.places, s32[4]{0:T(128)} %term_op.1, bf16[8,16,16]{2,1,0:T(8,128)(2,1)} %ops_ref.1, bf16[8,512,128]{2,1,0:T(8,128)(2,1)} %bitcast.5, ...), custom_call_target="tpu_custom_call" | custom-call | bytes 2097152 | tf_op jit(solution)/shard_map/pack/pallas_call | solution.py:145
  7.0 1.3 collective-permute-start.2
  8.8 1.0 copy-done.9
  9.9 1.3 collective-permute-start.1
  11.2 3.9 %collective-permute-done.2.received_ref = bf16[8,1,128,128]{3,2,1,0:T(8,128)(2,1)S(1)} collective-permute-done((bf16[8,1,128,128]{3,2,1,0:T(8,128)(2,1)}, bf16[8,1,128,128]{3,2,1,0:T(8,128)(2,1)S(1)}, u32[]{:S(2)}, u32[]{:S(2)}) %collective-permute-start.2) | collective-permute-done | bytes 262176 | tf_op jit(solution)/shard_map/ppermute | solution.py:578
  16.9 1.5 collective-permute-start.3
  18.5 1.0 copy-done.10
  19.6 13.6 %left.3 = (bf16[8,1,8,256,128]{4,3,2,1,0:T(8,128)(2,1)S(1)}, bf16[8,1,8,256,128]{4,3,2,1,0:T(8,128)(2,1)S(1)}, bf16[8,1,8,256,128]{4,3,2,1,0:T(8,128)(2,1)S(1)},...) custom-call(s32[4]{0:T(128)S(1)} %pad_add_fusion.meta, ...), custom_call_target="tpu_custom_call" | custom-call | flops 25165824 | bytes 16384 | tf_op jit(solution)/shard_map/left/pallas_call | solution.py:257
  33.2 2.0 %copy-done.5 = bf16[8,1,8,256,128]{4,3,2,1,0:T(8,128)(2,1)} copy-done((bf16[8,1,8,256,128]{4,3,2,1,0:T(8,128)(2,1)}, bf16[8,1,8,256,128]{4,3,2,1,0:T(8,128)(2,1)S(1)}, u32[]{:S(2)}) %copy-start.5) | copy-done | bytes 4194328
  35.2 1.3 collective-permute-start.5
  37.2 9.3 %left.4 = (bf16[8,1,8,256,128]{4,3,2,1,0:T(8,128)(2,1)S(1)}, bf16[8,1,8,256,128]{4,3,2,1,0:T(8,128)(2,1)S(1)}, bf16[8,1,8,256,128]{4,3,2,1,0:T(8,128)(2,1)S(1)}, f32[8,128]{1,0:T(8,128)S(1)}) custom-call(s32[4]{0:T(128)S(1)} %pad_add_fusion.meta, s32[8]{0:T(128)S(1)} %select_reduce_fusion.places, s32[32]{0:T(128)S(1)} %copy-done.13, ...), custom_call_target="tpu_custom_call" | custom-call | flops 9437184 | bytes 8192 | tf_op jit(solution)/shard_map/left/pallas_call | solution.py:257
  46.5 2.0 %copy-done.7 = bf16[8,1,8,256,128]{4,3,2,1,0:T(8,128)(2,1)} copy-done((bf16[8,1,8,256,128]{4,3,2,1,0:T(8,128)(2,1)}, bf16[8,1,8,256,128]{4,3,2,1,0:T(8,128)(2,1)S(1)}, u32[]{:S(2)}) %copy-start.7) | copy-done | bytes 4194328
  48.6 2.5 %collective-permute-done.5.rest_4_ = bf16[2,8,1,128,128]{4,3,2,1,0:T(8,128)(2,1)S(1)} collective-permute-done((bf16[2,8,1,128,128]{4,3,2,1,0:T(8,128)(2,1)}, bf16[2,8,1,128,128]{4,3,2,1,0:T(8,128)(2,1)S(1)}, u32[]{:S(2)}, u32[]{:S(2)}) %collective-permute-start.5) | collective-permute-done | bytes 524320 | tf_op jit(solution)/shard_map/ppermute | solution.py:620
  51.1 1.9 %choose.4 = (bf16[8,1,128,128]{3,2,1,0:T(8,128)(2,1)S(1)}, bf16[8,1,128,128]{3,2,1,0:T(8,128)(2,1)S(1)}) custom-call(s32[4]{0:T(128)S(1)} %pad_add_fusion.meta, s32[8]{0:T(128)S(1)} %select_reduce_fusion.places, s32[8,2]{1,0:T(8,128)S(1)} %copy.35.partners, f32[8,128]{1,0:T(8,128)S(1)} %get-tuple-element.43.rest_0_, ...), custom_call_target="tpu_custom_call" | custom-call | bytes 4096 | tf_op jit(solution)/shard_map/choose/pallas_call | solution.py:328
  54.3 1.4 collective-permute-start.10
  55.8 1.2 collective-permute-start.7
  57.1 13.0 %collective-permute-done.10.rest_5_ = bf16[2,8,1,128,128]{4,3,2,1,0:T(8,128)(2,1)S(1)} collective-permute-done((bf16[2,8,1,128,128]{4,3,2,1,0:T(8,128)(2,1)S(1)}, bf16[2,8,1,128,128]{4,3,2,1,0:T(8,128)(2,1)S(1)}, u32[]{:S(2)}, u32[]{:S(2)}) %collective-permute-start.10) | collective-permute-done | bytes 524320 | tf_op jit(solution)/shard_map/ppermute | solution.py:620
  70.0 1.3 choose.5
  72.9 1.3 collective-permute-start.14
  74.3 1.3 collective-permute-start.12
  75.5 14.7 %chunk.4 = (f32[8,16,128,128]{3,2,1,0:T(8,128)S(1)}, f32[8,128]{1,0:T(8,128)S(1)}) custom-call(s32[4]{0:T(128)S(1)} %pad_add_fusion.meta, s32[8]{0:T(128)S(1)} %select_reduce_fusion.places, s32[32]{0:T(128)S(1)} %copy-done.13, s32[8,2]{1,0:T(8,128)S(1)} %copy.35.partners, s32[8]{0:T(128)S(1)} %copy-done.12, ...), custom_call_target="tpu_custom_call" | custom-call | flops 13631488 | bytes 8192 | tf_op jit(solution)/shard_map/chunk/pallas_call | solution.py:454
  90.3 1.4 choose.6
  91.8 1.3 collective-permute-start.17
  94.1 13.3 %chunk.5 = (f32[8,16,128,128]{3,2,1,0:T(8,128)S(1)}, f32[8,128]{1,0:T(8,128)S(1)}) custom-call(s32[4]{0:T(128)S(1)} %pad_add_fusion.meta, s32[8]{0:T(128)S(1)} %select_reduce_fusion.places, s32[32]{0:T(128)S(1)} %copy-done.13, s32[8,2]{1,0:T(8,128)S(1)} %copy.35.partners, s32[8]{0:T(128)S(1)} %copy-done.12, ...), custom_call_target="tpu_custom_call", output_to_operand_aliasing={{0}: (13, {})} | custom-call | flops 10485760 | bytes 8192 | tf_op jit(solution)/shard_map/chunk/pallas_call | solution.py:454
  107.4 7.2 %left.5 = (bf16[8,1,8,256,128]{4,3,2,1,0:T(8,128)(2,1)S(1)}, bf16[8,1,8,256,128]{4,3,2,1,0:T(8,128)(2,1)S(1)}, f32[8,128]{1,0:T(8,128)S(1)}) custom-call(s32[4]{0:T(128)S(1)} %pad_add_fusion.meta, s32[8]{0:T(128)S(1)} %select_reduce_fusion.places, s32[32]{0:T(128)S(1)} %copy-done.13, s32[8,2]{1,0:T(8,128)S(1)} %copy.35.partners, s32[8]{0:T(128)S(1)} %copy-done.12, ...), custom_call_target="tpu_custom_call" | custom-call | flops 6291456 | bytes 8192 | tf_op jit(solution)/shard_map/left/pallas_call | solution.py:257
  114.7 1.3 choose.7
  117.9 13.3 %chunk.6 = (f32[8,16,128,128]{3,2,1,0:T(8,128)S(1)}, f32[8,128]{1,0:T(8,128)S(1)}) custom-call(s32[4]{0:T(128)S(1)} %pad_add_fusion.meta, s32[8]{0:T(128)S(1)} %select_reduce_fusion.places, s32[32]{0:T(128)S(1)} %copy-done.13, s32[8,2]{1,0:T(8,128)S(1)} %copy.35.partners, s32[8]{0:T(128)S(1)} %copy-done.12, ...), custom_call_target="tpu_custom_call", output_to_operand_aliasing={{0}: (13, {})} | custom-call | flops 10485760 | bytes 8192 | tf_op jit(solution)/shard_map/chunk/pallas_call | solution.py:454
  131.3 9.0 %chunk.7 = (bf16[8,16,128,128]{3,2,1,0:T(8,128)(2,1)S(1)}, f32[8,128]{1,0:T(8,128)S(1)}) custom-call(s32[4]{0:T(128)S(1)} %pad_add_fusion.meta, s32[8]{0:T(128)S(1)} %select_reduce_fusion.places, s32[32]{0:T(128)S(1)} %copy-done.13, s32[8,2]{1,0:T(8,128)S(1)} %copy.35.partners, s32[8]{0:T(128)S(1)} %copy-done.12, f32[8,128]{1,0:T(8,128)S(1)} %get-tuple-element.66.after_ref, ...), custom_call_target="tpu_custom_call" | custom-call | flops 4194304 | bytes 8192 | tf_op jit(solution)/shard_map/chunk/pallas_call | solution.py:454
  140.5 3.5 %collective-permute-start.23 = (f32[16,128]{1,0:T(8,128)S(1)}, f32[16,128]{1,0:T(8,128)S(1)}, u32[]{:S(2)}, u32[]{:S(2)}) collective-permute-start(f32[16,128]{1,0:T(8,128)S(1)} %constant_dynamic-update-slice_fusion), channel_id=1, source_target_pairs={{0,12},{4,8},{8,4},{12,0},{1,13},{5,9},{9,5},{13,1},{2,14},{6,10},... | collective-permute-start | bytes 24584 | tf_op jit(solution)/shard_map/ppermute | solution.py:578
  143.9 1.1 collective-permute-done.23
  145.1 1.8 %collective-permute-start.24 = (f32[16,128]{1,0:T(8,128)S(1)}, f32[16,128]{1,0:T(8,128)S(1)}, u32[]{:S(2)}, u32[]{:S(2)}) collective-permute-start(f32[16,128]{1,0:T(8,128)S(1)} %add_add_fusion), channel_id=1, source_target_pairs={{0,1},{1,0},{2,3},{3,2},{4,5},{5,4},{6,7},{7,6},{8,9},{9,8},{10,11... | collective-permute-start | bytes 24584 | tf_op jit(solution)/shard_map/ppermute | solution.py:578
  147.7 6.6 %residual.1 = (bf16[8,2,16,128,128]{4,3,2,1,0:T(8,128)(2,1)}, f32[1]{0:T(128)}) custom-call(s32[4]{0:T(128)S(1)} %pad_add_fusion.meta, s32[8]{0:T(128)S(1)} %select_reduce_fusion.places, s32[32]{0:T(128)S(1)} %copy-done.13, s32[8,2]{1,0:T(8,128)S(1)} %copy.35.partners, s32[8]{0:T(128)S(1)} %copy-done.12, f32[16,128]{1,0:T(8,128)S(1)} %add.48.folds_ref, ...), custom_call_target="tpu_custom_call" | custom-call | flops 12582912 | bytes 25165824 | tf_op jit(solution)/shard_map/residual/pallas_call | solution.py:532
  (84 shorter events, 12.8 us)
Async XLA Ops:
  0.6 17.9 %copy-start.13 = (s32[32]{0:T(128)S(1)}, s32[32]{0:T(128)}, u32[]{:S(2)}) copy-start(s32[32]{0:T(128)} %sector_rows.15) | copy-start | bytes 388
  0.6 17.9 %copy-start.12 = (s32[8]{0:T(128)S(1)}, s32[8]{0:T(128)}, u32[]{:S(2)}) copy-start(s32[8]{0:T(128)} %counts.15) | copy-start | bytes 100
  6.3 2.5 %collective-permute-start = (bf16[2112,128]{1,0:T(8,128)(2,1)}, bf16[2112,128]{1,0:T(8,128)(2,1)S(1)}, u32[]{:S(2)}, u32[]{:S(2)}) collective-permute-start(bf16[2112,128]{1,0:T(8,128)(2,1)} %get-tuple-element.40), channel_id=1, source_target_pairs={{0,1},{1,0},{2,3},{3,2},{4,5},{5,4},{6,7},{7,6},{8,9},{9,8},{10,11... | collective-permute-start | bytes 1622024 | tf_op jit(solution)/shard_map/ppermute | solution.py:578
  7.0 8.1 %collective-permute-start.2 = (bf16[8,1,128,128]{3,2,1,0:T(8,128)(2,1)}, bf16[8,1,128,128]{3,2,1,0:T(8,128)(2,1)S(1)}, u32[]{:S(2)}, u32[]{:S(2)}) collective-permute-start(bf16[8,1,128,128]{3,2,1,0:T(8,128)(2,1)} %get-tuple-element.44.near_ref), channel_id=1, source_target_pairs={{0,4},{4,0},{8,12},{12,8},{1,5},{5,1},{9,13},{13,9},{2,6},{6,2},{1... | collective-permute-start | bytes 786440 | tf_op jit(solution)/shard_map/ppermute | solution.py:578
  8.3 26.9 %collective-permute-start.4 = (bf16[8,3,128,128]{3,2,1,0:T(8,128)(2,1)}, bf16[8,3,128,128]{3,2,1,0:T(8,128)(2,1)S(1)}, u32[]{:S(2)}, u32[]{:S(2)}) collective-permute-start(bf16[8,3,128,128]{3,2,1,0:T(8,128)(2,1)} %get-tuple-element.49.near_ref), channel_id=1, source_target_pairs={{0,4},{4,0},{8,12},{12,8},{1,5},{5,1},{9,13},{13,9},{2,6},{6,2},{1... | collective-permute-start | bytes 2359304 | tf_op jit(solution)/shard_map/ppermute | solution.py:578
  9.9 41.2 %collective-permute-start.1 = (bf16[2,2112,128]{2,1,0:T(8,128)(2,1)S(1)}, bf16[2,2112,128]{2,1,0:T(8,128)(2,1)S(1)}, u32[]{:S(2)}, u32[]{:S(2)}) collective-permute-start(bf16[2,2112,128]{2,1,0:T(8,128)(2,1)S(1)} %stack.29.rest_0_), channel_id=1, source_target_pairs={{0,2},{1,3},{2,0},{3,1},{4,6},{5,7},{6,4},{7,5},{8,10},{9,11},{10,... | collective-permute-start | bytes 3244040 | tf_op jit(solution)/shard_map/ppermute | solution.py:578
  16.9 18.3 %collective-permute-start.3 = (bf16[2,8,1,128,128]{4,3,2,1,0:T(8,128)(2,1)}, bf16[2,8,1,128,128]{4,3,2,1,0:T(8,128)(2,1)}, u32[]{:S(2)}, u32[]{:S(2)}) collective-permute-start(bf16[2,8,1,128,128]{4,3,2,1,0:T(8,128)(2,1)} %stack.30.rest_2_), channel_id=1, source_target_pairs={{4,8},{8,4},{5,9},{9,5},{6,10},{10,6},{7,11},{11,7},{20,24},{24,20... | collective-permute-start | bytes 1572872 | tf_op jit(solution)/shard_map/ppermute | solution.py:606
  35.2 17.8 %copy-start.1 = (bf16[8,1,8,256,128]{4,3,2,1,0:T(8,128)(2,1)}, bf16[8,1,8,256,128]{4,3,2,1,0:T(8,128)(2,1)S(1)}, u32[]{:S(2)}) copy-start(bf16[8,1,8,256,128]{4,3,2,1,0:T(8,128)(2,1)S(1)} %get-tuple-element.57.rest_0_) | copy-start | bytes 12582916
  35.2 17.8 %copy-start.3 = (bf16[8,1,8,256,128]{4,3,2,1,0:T(8,128)(2,1)}, bf16[8,1,8,256,128]{4,3,2,1,0:T(8,128)(2,1)S(1)}, u32[]{:S(2)}) copy-start(bf16[8,1,8,256,128]{4,3,2,1,0:T(8,128)(2,1)S(1)} %get-tuple-element.53.rest_0_) | copy-start | bytes 12582916
  35.2 15.9 %collective-permute-start.5 = (bf16[2,8,1,128,128]{4,3,2,1,0:T(8,128)(2,1)}, bf16[2,8,1,128,128]{4,3,2,1,0:T(8,128)(2,1)S(1)}, u32[]{:S(2)}, u32[]{:S(2)}) collective-permute-start(bf16[2,8,1,128,128]{4,3,2,1,0:T(8,128)(2,1)} %collective-permute-done.3.rest_3_), channel_id=1, source_target_pairs={{4,0},{8,12},{5,1},{9,13},{6,2},{10,14},{7,3},{11,15},{20,16},{24,... | collective-permute-start | bytes 1572872 | tf_op jit(solution)/shard_map/ppermute | solution.py:620
  36.5 17.8 %collective-permute-start.9 = (bf16[2,8,1,128,128]{4,3,2,1,0:T(8,128)(2,1)S(1)}, bf16[2,8,1,128,128]{4,3,2,1,0:T(8,128)(2,1)S(1)}, u32[]{:S(2)}, u32[]{:S(2)}) collective-permute-start(bf16[2,8,1,128,128]{4,3,2,1,0:T(8,128)(2,1)S(1)} %stack.33.rest_3_), channel_id=1, source_target_pairs={{4,8},{8,4},{5,9},{9,5},{6,10},{10,6},{7,11},{11,7},{20,24},{24,20... | collective-permute-start | bytes 1572872 | tf_op jit(solution)/shard_map/ppermute | solution.py:606
  53.0 2.8 %collective-permute-start.6 = (bf16[8,1,128,128]{3,2,1,0:T(8,128)(2,1)S(1)}, bf16[8,1,128,128]{3,2,1,0:T(8,128)(2,1)S(1)}, u32[]{:S(2)}, u32[]{:S(2)}) collective-permute-start(bf16[8,1,128,128]{3,2,1,0:T(8,128)(2,1)S(1)} %get-tuple-element.48), channel_id=1, source_target_pairs={{0,1},{1,0},{2,3},{3,2},{4,5},{5,4},{6,7},{7,6},{8,9},{9,8},{10,11... | collective-permute-start | bytes 786440 | tf_op jit(solution)/shard_map/ppermute | solution.py:578
  53.5 22.1 %copy-start.4 = (bf16[8,1,8,256,128]{4,3,2,1,0:T(8,128)(2,1)S(1)}, bf16[8,1,8,256,128]{4,3,2,1,0:T(8,128)(2,1)}, u32[]{:S(2)}) copy-start(bf16[8,1,8,256,128]{4,3,2,1,0:T(8,128)(2,1)} %copy-done.3) | copy-start | bytes 12582916
  53.5 3.6 %collective-permute-start.8 = (bf16[2,8,1,128,128]{4,3,2,1,0:T(8,128)(2,1)S(1)}, bf16[2,8,1,128,128]{4,3,2,1,0:T(8,128)(2,1)S(1)}, u32[]{:S(2)}, u32[]{:S(2)}) collective-permute-start(bf16[2,8,1,128,128]{4,3,2,1,0:T(8,128)(2,1)S(1)} %stack.32.rest_3_), channel_id=1, source_target_pairs={{4,8},{8,4},{5,9},{9,5},{6,10},{10,6},{7,11},{11,7},{20,24},{24,20... | collective-permute-start | bytes 1572872 | tf_op jit(solution)/shard_map/ppermute | solution.py:606
  54.3 15.7 %collective-permute-start.10 = (bf16[2,8,1,128,128]{4,3,2,1,0:T(8,128)(2,1)S(1)}, bf16[2,8,1,128,128]{4,3,2,1,0:T(8,128)(2,1)S(1)}, u32[]{:S(2)}, u32[]{:S(2)}) collective-permute-start(bf16[2,8,1,128,128]{4,3,2,1,0:T(8,128)(2,1)S(1)} %collective-permute-done.9.rest_4_), channel_id=1, source_target_pairs={{4,0},{8,12},{5,1},{9,13},{6,2},{10,14},{7,3},{11,15},{20,16},{24,... | collective-permute-start | bytes 1572872 | tf_op jit(solution)/shard_map/ppermute | solution.py:620
  55.8 14.2 %collective-permute-start.7 = (bf16[2,8,1,128,128]{4,3,2,1,0:T(8,128)(2,1)S(1)}, bf16[2,8,1,128,128]{4,3,2,1,0:T(8,128)(2,1)S(1)}, u32[]{:S(2)}, u32[]{:S(2)}) collective-permute-start(bf16[2,8,1,128,128]{4,3,2,1,0:T(8,128)(2,1)S(1)} %stack.31.rest_0_), channel_id=1, source_target_pairs={{0,2},{1,3},{2,0},{3,1},{4,6},{5,7},{6,4},{7,5},{8,10},{9,11},{10,... | collective-permute-start | bytes 1572872 | tf_op jit(solution)/shard_map/ppermute | solution.py:578
  71.3 2.9 %collective-permute-start.11 = (bf16[8,1,128,128]{3,2,1,0:T(8,128)(2,1)S(1)}, bf16[8,1,128,128]{3,2,1,0:T(8,128)(2,1)S(1)}, u32[]{:S(2)}, u32[]{:S(2)}) collective-permute-start(bf16[8,1,128,128]{3,2,1,0:T(8,128)(2,1)S(1)} %get-tuple-element.52), channel_id=1, source_target_pairs={{0,1},{1,0},{2,3},{3,2},{4,5},{5,4},{6,7},{7,6},{8,9},{9,8},{10,11... | collective-permute-start | bytes 786440 | tf_op jit(solution)/shard_map/ppermute | solution.py:578
  72.2 18.1 %collective-permute-start.13 = (bf16[2,8,1,128,128]{4,3,2,1,0:T(8,128)(2,1)S(1)}, bf16[2,8,1,128,128]{4,3,2,1,0:T(8,128)(2,1)S(1)}, u32[]{:S(2)}, u32[]{:S(2)}) collective-permute-start(bf16[2,8,1,128,128]{4,3,2,1,0:T(8,128)(2,1)S(1)} %stack.35.rest_2_), channel_id=1, source_target_pairs={{4,8},{8,4},{5,9},{9,5},{6,10},{10,6},{7,11},{11,7},{20,24},{24,20... | collective-permute-start | bytes 1572872 | tf_op jit(solution)/shard_map/ppermute | solution.py:606
  72.9 17.4 %collective-permute-start.14 = (bf16[2,8,1,128,128]{4,3,2,1,0:T(8,128)(2,1)S(1)}, bf16[2,8,1,128,128]{4,3,2,1,0:T(8,128)(2,1)S(1)}, u32[]{:S(2)}, u32[]{:S(2)}) collective-permute-start(bf16[2,8,1,128,128]{4,3,2,1,0:T(8,128)(2,1)S(1)} %collective-permute-done.8.rest_2_.rest_4_), channel_id=1, source_target_pairs={{4,0},{8,12},{5,1},{9,13},{6,2},{10,14},{7,3},{11,15},{20,16},{24,... | collective-permute-start | bytes 1572872 | tf_op jit(solution)/shard_map/ppermute | solution.py:620
  74.3 16.0 %collective-permute-start.12 = (bf16[2,8,1,128,128]{4,3,2,1,0:T(8,128)(2,1)S(1)}, bf16[2,8,1,128,128]{4,3,2,1,0:T(8,128)(2,1)S(1)}, u32[]{:S(2)}, u32[]{:S(2)}) collective-permute-start(bf16[2,8,1,128,128]{4,3,2,1,0:T(8,128)(2,1)S(1)} %stack.34.after_ref), channel_id=1, source_target_pairs={{0,2},{1,3},{2,0},{3,1},{4,6},{5,7},{6,4},{7,5},{8,10},{9,11},{10,... | collective-permute-start | bytes 1572872 | tf_op jit(solution)/shard_map/ppermute | solution.py:578
  75.5 18.5 %copy-start.2 = (bf16[8,1,8,256,128]{4,3,2,1,0:T(8,128)(2,1)S(1)}, bf16[8,1,8,256,128]{4,3,2,1,0:T(8,128)(2,1)}, u32[]{:S(2)}) copy-start(bf16[8,1,8,256,128]{4,3,2,1,0:T(8,128)(2,1)} %copy-done.1) | copy-start | bytes 12582916
  91.8 1.6 %collective-permute-start.15 = (bf16[8,1,128,128]{3,2,1,0:T(8,128)(2,1)S(1)}, bf16[8,1,128,128]{3,2,1,0:T(8,128)(2,1)S(1)}, u32[]{:S(2)}, u32[]{:S(2)}) collective-permute-start(bf16[8,1,128,128]{3,2,1,0:T(8,128)(2,1)S(1)} %get-tuple-element.56), channel_id=1, source_target_pairs={{0,1},{1,0},{2,3},{3,2},{4,5},{5,4},{6,7},{7,6},{8,9},{9,8},{10,11... | collective-permute-start | bytes 786440 | tf_op jit(solution)/shard_map/ppermute | solution.py:578
  91.8 22.8 %collective-permute-start.17 = (bf16[2,8,1,128,128]{4,3,2,1,0:T(8,128)(2,1)S(1)}, bf16[2,8,1,128,128]{4,3,2,1,0:T(8,128)(2,1)S(1)}, u32[]{:S(2)}, u32[]{:S(2)}) collective-permute-start(bf16[2,8,1,128,128]{4,3,2,1,0:T(8,128)(2,1)S(1)} %collective-permute-done.13.rest_2_.rest_3_), channel_id=1, source_target_pairs={{4,0},{8,12},{5,1},{9,13},{6,2},{10,14},{7,3},{11,15},{20,16},{24,... | collective-permute-start | bytes 1572872 | tf_op jit(solution)/shard_map/ppermute | solution.py:620
  93.4 21.3 %collective-permute-start.16 = (bf16[2,8,1,128,128]{4,3,2,1,0:T(8,128)(2,1)S(1)}, bf16[2,8,1,128,128]{4,3,2,1,0:T(8,128)(2,1)S(1)}, u32[]{:S(2)}, u32[]{:S(2)}) collective-permute-start(bf16[2,8,1,128,128]{4,3,2,1,0:T(8,128)(2,1)S(1)} %stack.36.after_ref), channel_id=1, source_target_pairs={{0,2},{1,3},{2,0},{3,1},{4,6},{5,7},{6,4},{7,5},{8,10},{9,11},{10,... | collective-permute-start | bytes 1572872 | tf_op jit(solution)/shard_map/ppermute | solution.py:578
  115.9 15.2 %collective-permute-start.19 = (bf16[8,1,128,128]{3,2,1,0:T(8,128)(2,1)S(1)}, bf16[8,1,128,128]{3,2,1,0:T(8,128)(2,1)S(1)}, u32[]{:S(2)}, u32[]{:S(2)}) collective-permute-start(bf16[8,1,128,128]{3,2,1,0:T(8,128)(2,1)S(1)} %get-tuple-element.62.after_ref.rest_4_), channel_id=1, source_target_pairs={{0,2},{1,3},{2,0},{3,1},{4,6},{5,7},{6,4},{7,5},{8,10},{9,11},{10,... | collective-permute-start | bytes 786440 | tf_op jit(solution)/shard_map/ppermute | solution.py:578
  116.8 14.3 %collective-permute-start.20 = (bf16[8,1,128,128]{3,2,1,0:T(8,128)(2,1)S(1)}, bf16[8,1,128,128]{3,2,1,0:T(8,128)(2,1)S(1)}, u32[]{:S(2)}, u32[]{:S(2)}) collective-permute-start(bf16[8,1,128,128]{3,2,1,0:T(8,128)(2,1)S(1)} %get-tuple-element.71), channel_id=1, source_target_pairs={{0,3},{1,2},{2,1},{3,0},{4,7},{5,6},{6,5},{7,4},{8,11},{9,10},{10,... | collective-permute-start | bytes 786440 | tf_op jit(solution)/shard_map/ppermute | solution.py:578
  116.8 14.4 %collective-permute-start.18 = (bf16[8,1,128,128]{3,2,1,0:T(8,128)(2,1)S(1)}, bf16[8,1,128,128]{3,2,1,0:T(8,128)(2,1)S(1)}, u32[]{:S(2)}, u32[]{:S(2)}) collective-permute-start(bf16[8,1,128,128]{3,2,1,0:T(8,128)(2,1)S(1)} %get-tuple-element.71), channel_id=1, source_target_pairs={{0,1},{1,0},{2,3},{3,2},{4,5},{5,4},{6,7},{7,6},{8,9},{9,8},{10,11... | collective-permute-start | bytes 786440 | tf_op jit(solution)/shard_map/ppermute | solution.py:578
  140.2 7.5 %collective-permute-start.25 = (bf16[8,16,128,128]{3,2,1,0:T(8,128)(2,1)S(1)}, bf16[8,16,128,128]{3,2,1,0:T(8,128)(2,1)S(1)}, u32[]{:S(2)}, u32[]{:S(2)}) collective-permute-start(bf16[8,16,128,128]{3,2,1,0:T(8,128)(2,1)S(1)} %get-tuple-element.75.own_ref), channel_id=1, source_target_pairs={{0,1},{1,0},{2,3},{3,2},{4,5},{5,4},{6,7},{7,6},{8,9},{9,8},{10,11... | collective-permute-start | bytes 12582920 | tf_op jit(solution)/shard_map/ppermute | solution.py:578
  140.3 3.6 %collective-permute-start.21 = (f32[16,128]{1,0:T(8,128)S(1)}, f32[16,128]{1,0:T(8,128)S(1)}, u32[]{:S(2)}, u32[]{:S(2)}) collective-permute-start(f32[16,128]{1,0:T(8,128)S(1)} %constant_dynamic-update-slice_fusion), channel_id=1, source_target_pairs={{0,4},{4,0},{8,12},{12,8},{1,5},{5,1},{9,13},{13,9},{2,6},{6,2},{1... | collective-permute-start | bytes 24584 | tf_op jit(solution)/shard_map/ppermute | solution.py:578
  140.4 3.5 %collective-permute-start.22 = (f32[16,128]{1,0:T(8,128)S(1)}, f32[16,128]{1,0:T(8,128)S(1)}, u32[]{:S(2)}, u32[]{:S(2)}) collective-permute-start(f32[16,128]{1,0:T(8,128)S(1)} %constant_dynamic-update-slice_fusion), channel_id=1, source_target_pairs={{0,8},{4,12},{8,0},{12,4},{1,9},{5,13},{9,1},{13,5},{2,10},{6,14},... | collective-permute-start | bytes 24584 | tf_op jit(solution)/shard_map/ppermute | solution.py:578
  140.5 4.6 %collective-permute-start.23 = (f32[16,128]{1,0:T(8,128)S(1)}, f32[16,128]{1,0:T(8,128)S(1)}, u32[]{:S(2)}, u32[]{:S(2)}) collective-permute-start(f32[16,128]{1,0:T(8,128)S(1)} %constant_dynamic-update-slice_fusion), channel_id=1, source_target_pairs={{0,12},{4,8},{8,4},{12,0},{1,13},{5,9},{9,5},{13,1},{2,14},{6,10},... | collective-permute-start | bytes 24584 | tf_op jit(solution)/shard_map/ppermute | solution.py:578
  145.1 2.7 %collective-permute-start.24 = (f32[16,128]{1,0:T(8,128)S(1)}, f32[16,128]{1,0:T(8,128)S(1)}, u32[]{:S(2)}, u32[]{:S(2)}) collective-permute-start(f32[16,128]{1,0:T(8,128)S(1)} %add_add_fusion), channel_id=1, source_target_pairs={{0,1},{1,0},{2,3},{3,2},{4,5},{5,4},{6,7},{7,6},{8,9},{9,8},{10,11... | collective-permute-start | bytes 24584 | tf_op jit(solution)/shard_map/ppermute | solution.py:578
  (9 other events, 68.4 us)
where the time goes:
time: 156 us; the launch traced here: 155 us
  Pallas kernels  97.8 us (63%)
  starting transfers between devices  24.5 us (16%)
  waiting for transfers between devices  21.9 us (14%)
  local copies, waits for them, and re-layouts  7.82 us (5%)
    pallas_call x4, Pallas kernels, chunk_call(): pl.pallas_call(functools.partial(chunk_kernel, first, last, held, chunk,...  50.3 us
    pallas_call x3, Pallas kernels, left_call(): pl.pallas_call(functools.partial(left_kernel, first, held, items, len(pay...  30.1 us
    ppermute x4, waiting for transfers between devices, choose(): pieces = pieces + [lax.ppermute(pieces[-1], 'sec', [(1, 0), (2, 3)])]  15.5 us
    ppermute x18, starting transfers between devices, swap(): return lax.ppermute(value, axis, [(i, i ^ bits) for i in range(size)])  15.5 us
    unnamed x32, local copies, waits for them, and re-layouts  7.16 us
    pallas_call x1, Pallas kernels, residual_call(): pl.pallas_call(functools.partial(residual_kernel, sectors // 2, slots), i...  6.6 us
    ppermute x18, waiting for transfers between devices, swap(): return lax.ppermute(value, axis, [(i, i ^ bits) for i in range(size)])  6.42 us
    pallas_call x4, Pallas kernels, choose_call(): pl.pallas_call(functools.partial(choose_kernel, line, len(pieces), len(af...  5.85 us
  transfers between devices with their start and end apart: 26, of which 7 were waited for; matrix products, arithmetic and copies ran while one was open for 0% of the time, Pallas kernels for 48%

commit v1 on v0

--- a/solution.py
+++ b/solution.py
@@ -660,6 +660,7 @@
         gather()
     token, = go_left((1,), every[1:], token)
     token = choose(token)
+    token, = go_left(far, [len(chunks) - 1], token)
     total = None
     for at, chunk in enumerate(chunks):
         last = at == len(chunks) - 1
@@ -673,8 +674,6 @@
             [products.pop((at, source)) for source in ahead], payloads,
             rights[at], total, token,
         )
-        if at == len(chunks) - 3:
-            token, = go_left(far, [len(chunks) - 1], token)
 
     other = swap(total, 1)
     folds = jnp.concatenate([token, squares], axis=0)

time: 156 us -> 146 us (0.936)
  the two profiles are of different devices: /device:TPU:5 before, /device:TPU:0 now
where the time goes in v1:
time: 146 us; the launch traced here: 145 us
  Pallas kernels  86.5 us (59%)
  starting transfers between devices  26 us (18%)
  waiting for transfers between devices  22.3 us (15%)
  local copies, waits for them, and re-layouts  7.78 us (5%)
    pallas_call x4, Pallas kernels, chunk_call(): pl.pallas_call(functools.partial(chunk_kernel, first, last, held, chunk,...  43 us
    pallas_call x3, Pallas kernels, left_call(): pl.pallas_call(functools.partial(left_kernel, first, held, items, len(pay...  26.1 us
    ppermute x18, starting transfers between devices, swap(): return lax.ppermute(value, axis, [(i, i ^ bits) for i in range(size)])  17.1 us
    ppermute x4, waiting for transfers between devices, choose(): pieces = pieces + [lax.ppermute(pieces[-1], 'sec', [(1, 0), (2, 3)])]  14.6 us
    ppermute x18, waiting for transfers between devices, swap(): return lax.ppermute(value, axis, [(i, i ^ bits) for i in range(size)])  7.68 us
    unnamed x44, local copies, waits for them, and re-layouts  7.12 us
    pallas_call x1, Pallas kernels, residual_call(): pl.pallas_call(functools.partial(residual_kernel, sectors // 2, slots), i...  6.6 us
    pallas_call x4, Pallas kernels, choose_call(): pl.pallas_call(functools.partial(choose_kernel, line, len(pieces), len(af...  5.88 us
  transfers between devices with their start and end apart: 26, of which 9 were waited for; matrix products, arithmetic and copies ran while one was open for 0% of the time, Pallas kernels for 44%

profile of v1, /device:TPU:0, one launch (start us, length us, event | category | flops | bytes accessed | tf_op | source)
XLA Modules:
  0.0 145.1 jit_solution(16340208186028309048)
XLA Ops:
  2.5 3.8 %pack.1 = (bf16[2112,128]{1,0:T(8,128)(2,1)}, bf16[2112,128]{1,0:T(8,128)(2,1)}, bf16[8,1,128,128]{3,2,1,0:T(8,128)(2,1)}, bf16[8,3,128,128]{3,2,1,0:T(8,128)(2,1)}) custom-call(s32[8]{0:T(128)} %dynamic_slice.8.places, s32[4]{0:T(128)} %term_op.1, bf16[8,16,16]{2,1,0:T(8,128)(2,1)} %ops_ref.1, bf16[8,512,128]{2,1,0:T(8,128)(2,1)} %bitcast.5, ...), custom_call_target="tpu_custom_call" | custom-call | bytes 2097152 | tf_op jit(solution)/shard_map/pack/pallas_call | solution.py:145
  6.8 2.6 %collective-permute-start.2 = (bf16[8,1,128,128]{3,2,1,0:T(8,128)(2,1)}, bf16[8,1,128,128]{3,2,1,0:T(8,128)(2,1)S(1)}, u32[]{:S(2)}, u32[]{:S(2)}) collective-permute-start(bf16[8,1,128,128]{3,2,1,0:T(8,128)(2,1)} %get-tuple-element.44.near_ref), channel_id=1, source_target_pairs={{0,4},{4,0},{8,12},{12,8},{1,5},{5,1},{9,13},{13,9},{2,6},{6,2},{1... | collective-permute-start | bytes 786440 | tf_op jit(solution)/shard_map/ppermute | solution.py:578
  10.6 1.9 %collective-permute-start.1 = (bf16[2,2112,128]{2,1,0:T(8,128)(2,1)S(1)}, bf16[2,2112,128]{2,1,0:T(8,128)(2,1)S(1)}, u32[]{:S(2)}, u32[]{:S(2)}) collective-permute-start(bf16[2,2112,128]{2,1,0:T(8,128)(2,1)S(1)} %stack.29.rest_0_), channel_id=1, source_target_pairs={{0,2},{1,3},{2,0},{3,1},{4,6},{5,7},{6,4},{7,5},{8,10},{9,11},{10,... | collective-permute-start | bytes 3244040 | tf_op jit(solution)/shard_map/ppermute | solution.py:578
  12.6 4.2 %collective-permute-done.2.received_ref = bf16[8,1,128,128]{3,2,1,0:T(8,128)(2,1)S(1)} collective-permute-done((bf16[8,1,128,128]{3,2,1,0:T(8,128)(2,1)}, bf16[8,1,128,128]{3,2,1,0:T(8,128)(2,1)S(1)}, u32[]{:S(2)}, u32[]{:S(2)}) %collective-permute-start.2) | collective-permute-done | bytes 262176 | tf_op jit(solution)/shard_map/ppermute | solution.py:578
  18.6 1.5 %collective-permute-start.3 = (bf16[2,8,1,128,128]{4,3,2,1,0:T(8,128)(2,1)}, bf16[2,8,1,128,128]{4,3,2,1,0:T(8,128)(2,1)}, u32[]{:S(2)}, u32[]{:S(2)}) collective-permute-start(bf16[2,8,1,128,128]{4,3,2,1,0:T(8,128)(2,1)} %stack.30.rest_2_), channel_id=1, source_target_pairs={{4,8},{8,4},{5,9},{9,5},{6,10},{10,6},{7,11},{11,7},{20,24},{24,20... | collective-permute-start | bytes 1572872 | tf_op jit(solution)/shard_map/ppermute | solution.py:606
  21.2 11.7 %left.3 = (bf16[8,1,8,256,128]{4,3,2,1,0:T(8,128)(2,1)S(1)}, bf16[8,1,8,256,128]{4,3,2,1,0:T(8,128)(2,1)S(1)}, bf16[8,1,8,256,128]{4,3,2,1,0:T(8,128)(2,1)S(1)},...) custom-call(s32[4]{0:T(128)S(1)} %pad_add_fusion.meta, ...), custom_call_target="tpu_custom_call" | custom-call | flops 25165824 | bytes 16384 | tf_op jit(solution)/shard_map/left/pallas_call | solution.py:257
  33.0 2.0 %copy-done.7 = bf16[8,1,8,256,128]{4,3,2,1,0:T(8,128)(2,1)} copy-done((bf16[8,1,8,256,128]{4,3,2,1,0:T(8,128)(2,1)}, bf16[8,1,8,256,128]{4,3,2,1,0:T(8,128)(2,1)S(1)}, u32[]{:S(2)}) %copy-start.7) | copy-done | bytes 4194328
  35.0 1.3 collective-permute-start.5
  37.0 8.1 %left.4 = (bf16[8,1,8,256,128]{4,3,2,1,0:T(8,128)(2,1)S(1)}, bf16[8,1,8,256,128]{4,3,2,1,0:T(8,128)(2,1)S(1)}, bf16[8,1,8,256,128]{4,3,2,1,0:T(8,128)(2,1)S(1)}, f32[8,128]{1,0:T(8,128)S(1)}) custom-call(s32[4]{0:T(128)S(1)} %pad_add_fusion.meta, s32[8]{0:T(128)S(1)} %select_reduce_fusion.places, s32[32]{0:T(128)S(1)} %copy-done.19, ...), custom_call_target="tpu_custom_call" | custom-call | flops 9437184 | bytes 8192 | tf_op jit(solution)/shard_map/left/pallas_call | solution.py:257
  45.2 5.6 %collective-permute-done.5.rest_4_ = bf16[2,8,1,128,128]{4,3,2,1,0:T(8,128)(2,1)S(1)} collective-permute-done((bf16[2,8,1,128,128]{4,3,2,1,0:T(8,128)(2,1)}, bf16[2,8,1,128,128]{4,3,2,1,0:T(8,128)(2,1)S(1)}, u32[]{:S(2)}, u32[]{:S(2)}) %collective-permute-start.5) | collective-permute-done | bytes 524320 | tf_op jit(solution)/shard_map/ppermute | solution.py:620
  50.8 1.9 %choose.4 = (bf16[8,1,128,128]{3,2,1,0:T(8,128)(2,1)S(1)}, bf16[8,1,128,128]{3,2,1,0:T(8,128)(2,1)S(1)}) custom-call(s32[4]{0:T(128)S(1)} %pad_add_fusion.meta, s32[8]{0:T(128)S(1)} %select_reduce_fusion.places, s32[8,2]{1,0:T(8,128)S(1)} %copy.35.partners, f32[8,128]{1,0:T(8,128)S(1)} %get-tuple-element.43.rest_0_, ...), custom_call_target="tpu_custom_call" | custom-call | bytes 4096 | tf_op jit(solution)/shard_map/choose/pallas_call | solution.py:328
  53.5 1.3 collective-permute-start.10
  54.9 1.5 %collective-permute-start.7 = (bf16[2,8,1,128,128]{4,3,2,1,0:T(8,128)(2,1)S(1)}, bf16[2,8,1,128,128]{4,3,2,1,0:T(8,128)(2,1)S(1)}, u32[]{:S(2)}, u32[]{:S(2)}) collective-permute-start(bf16[2,8,1,128,128]{4,3,2,1,0:T(8,128)(2,1)S(1)} %stack.31.rest_0_), channel_id=1, source_target_pairs={{0,2},{1,3},{2,0},{3,1},{4,6},{5,7},{6,4},{7,5},{8,10},{9,11},{10,... | collective-permute-start | bytes 1572872 | tf_op jit(solution)/shard_map/ppermute | solution.py:578
  56.4 6.3 %left.5 = (bf16[8,1,8,256,128]{4,3,2,1,0:T(8,128)(2,1)S(1)}, bf16[8,1,8,256,128]{4,3,2,1,0:T(8,128)(2,1)S(1)}, f32[8,128]{1,0:T(8,128)S(1)}) custom-call(s32[4]{0:T(128)S(1)} %pad_add_fusion.meta, s32[8]{0:T(128)S(1)} %select_reduce_fusion.places, s32[32]{0:T(128)S(1)} %copy-done.19, s32[8,2]{1,0:T(8,128)S(1)} %copy.35.partners, s32[8]{0:T(128)S(1)} %copy-done.18, ...), custom_call_target="tpu_custom_call" | custom-call | flops 6291456 | bytes 8192 | tf_op jit(solution)/shard_map/left/pallas_call | solution.py:257
  62.7 2.0 %copy-done.11 = bf16[8,1,8,256,128]{4,3,2,1,0:T(8,128)(2,1)} copy-done((bf16[8,1,8,256,128]{4,3,2,1,0:T(8,128)(2,1)}, bf16[8,1,8,256,128]{4,3,2,1,0:T(8,128)(2,1)S(1)}, u32[]{:S(2)}) %copy-start.11) | copy-done | bytes 4194328
  64.7 5.1 %collective-permute-done.10.rest_5_ = bf16[2,8,1,128,128]{4,3,2,1,0:T(8,128)(2,1)S(1)} collective-permute-done((bf16[2,8,1,128,128]{4,3,2,1,0:T(8,128)(2,1)S(1)}, bf16[2,8,1,128,128]{4,3,2,1,0:T(8,128)(2,1)S(1)}, u32[]{:S(2)}, u32[]{:S(2)}) %collective-permute-start.10) | collective-permute-done | bytes 524320 | tf_op jit(solution)/shard_map/ppermute | solution.py:620
  69.9 1.3 choose.5
  72.0 1.5 %collective-permute-start.14 = (bf16[2,8,1,128,128]{4,3,2,1,0:T(8,128)(2,1)S(1)}, bf16[2,8,1,128,128]{4,3,2,1,0:T(8,128)(2,1)S(1)}, u32[]{:S(2)}, u32[]{:S(2)}) collective-permute-start(bf16[2,8,1,128,128]{4,3,2,1,0:T(8,128)(2,1)S(1)} %collective-permute-done.8.rest_2_.rest_4_), channel_id=1, source_target_pairs={{4,0},{8,12},{5,1},{9,13},{6,2},{10,14},{7,3},{11,15},{20,16},{24,... | collective-permute-start | bytes 1572872 | tf_op jit(solution)/shard_map/ppermute | solution.py:620
  73.5 1.5 %collective-permute-start.12 = (bf16[2,8,1,128,128]{4,3,2,1,0:T(8,128)(2,1)S(1)}, bf16[2,8,1,128,128]{4,3,2,1,0:T(8,128)(2,1)S(1)}, u32[]{:S(2)}, u32[]{:S(2)}) collective-permute-start(bf16[2,8,1,128,128]{4,3,2,1,0:T(8,128)(2,1)S(1)} %stack.34.after_ref), channel_id=1, source_target_pairs={{0,2},{1,3},{2,0},{3,1},{4,6},{5,7},{6,4},{7,5},{8,10},{9,11},{10,... | collective-permute-start | bytes 1572872 | tf_op jit(solution)/shard_map/ppermute | solution.py:578
  75.0 12.6 %chunk.4 = (f32[8,16,128,128]{3,2,1,0:T(8,128)S(1)}, f32[8,128]{1,0:T(8,128)S(1)}) custom-call(s32[4]{0:T(128)S(1)} %pad_add_fusion.meta, s32[8]{0:T(128)S(1)} %select_reduce_fusion.places, s32[32]{0:T(128)S(1)} %copy-done.19, s32[8,2]{1,0:T(8,128)S(1)} %copy.35.partners, s32[8]{0:T(128)S(1)} %copy-done.18, ...), custom_call_target="tpu_custom_call" | custom-call | flops 13631488 | bytes 8192 | tf_op jit(solution)/shard_map/chunk/pallas_call | solution.py:454
  87.6 2.1 %collective-permute-done.14.rest_5_ = bf16[2,8,1,128,128]{4,3,2,1,0:T(8,128)(2,1)S(1)} collective-permute-done((bf16[2,8,1,128,128]{4,3,2,1,0:T(8,128)(2,1)S(1)}, bf16[2,8,1,128,128]{4,3,2,1,0:T(8,128)(2,1)S(1)}, u32[]{:S(2)}, u32[]{:S(2)}) %collective-permute-start.14) | collective-permute-done | bytes 524320 | tf_op jit(solution)/shard_map/ppermute | solution.py:620
  91.0 1.3 collective-permute-start.17
  92.6 1.5 %collective-permute-start.16 = (bf16[2,8,1,128,128]{4,3,2,1,0:T(8,128)(2,1)S(1)}, bf16[2,8,1,128,128]{4,3,2,1,0:T(8,128)(2,1)S(1)}, u32[]{:S(2)}, u32[]{:S(2)}) collective-permute-start(bf16[2,8,1,128,128]{4,3,2,1,0:T(8,128)(2,1)S(1)} %stack.36.after_ref), channel_id=1, source_target_pairs={{0,2},{1,3},{2,0},{3,1},{4,6},{5,7},{6,4},{7,5},{8,10},{9,11},{10,... | collective-permute-start | bytes 1572872 | tf_op jit(solution)/shard_map/ppermute | solution.py:578
  94.1 11.3 %chunk.5 = (f32[8,16,128,128]{3,2,1,0:T(8,128)S(1)}, f32[8,128]{1,0:T(8,128)S(1)}) custom-call(s32[4]{0:T(128)S(1)} %pad_add_fusion.meta, s32[8]{0:T(128)S(1)} %select_reduce_fusion.places, s32[32]{0:T(128)S(1)} %copy-done.19, s32[8,2]{1,0:T(8,128)S(1)} %copy.35.partners, s32[8]{0:T(128)S(1)} %copy-done.18, ...), custom_call_target="tpu_custom_call", output_to_operand_aliasing={{0}: (13, {})} | custom-call | flops 10485760 | bytes 8192 | tf_op jit(solution)/shard_map/chunk/pallas_call | solution.py:454
  105.4 1.8 %collective-permute-done.17.rest_4_ = bf16[2,8,1,128,128]{4,3,2,1,0:T(8,128)(2,1)S(1)} collective-permute-done((bf16[2,8,1,128,128]{4,3,2,1,0:T(8,128)(2,1)S(1)}, bf16[2,8,1,128,128]{4,3,2,1,0:T(8,128)(2,1)S(1)}, u32[]{:S(2)}, u32[]{:S(2)}) %collective-permute-start.17) | collective-permute-done | bytes 524320 | tf_op jit(solution)/shard_map/ppermute | solution.py:620
  107.2 1.5 %choose.7 = (bf16[8,1,128,128]{3,2,1,0:T(8,128)(2,1)S(1)}, bf16[8,1,128,128]{3,2,1,0:T(8,128)(2,1)S(1)}) custom-call(s32[4]{0:T(128)S(1)} %pad_add_fusion.meta, s32[8]{0:T(128)S(1)} %select_reduce_fusion.places, s32[8,2]{1,0:T(8,128)S(1)} %copy.35.partners, f32[8,128]{1,0:T(8,128)S(1)} %get-tuple-element.61.rest_0_, ...), custom_call_target="tpu_custom_call" | custom-call | bytes 4096 | tf_op jit(solution)/shard_map/choose/pallas_call | solution.py:328
  108.7 1.5 %collective-permute-start.19 = (bf16[8,1,128,128]{3,2,1,0:T(8,128)(2,1)S(1)}, bf16[8,1,128,128]{3,2,1,0:T(8,128)(2,1)S(1)}, u32[]{:S(2)}, u32[]{:S(2)}) collective-permute-start(bf16[8,1,128,128]{3,2,1,0:T(8,128)(2,1)S(1)} %get-tuple-element.62.after_ref.rest_4_), channel_id=1, source_target_pairs={{0,2},{1,3},{2,0},{3,1},{4,6},{5,7},{6,4},{7,5},{8,10},{9,11},{10,... | collective-permute-start | bytes 786440 | tf_op jit(solution)/shard_map/ppermute | solution.py:578
  111.0 11.3 %chunk.6 = (f32[8,16,128,128]{3,2,1,0:T(8,128)S(1)}, f32[8,128]{1,0:T(8,128)S(1)}) custom-call(s32[4]{0:T(128)S(1)} %pad_add_fusion.meta, s32[8]{0:T(128)S(1)} %select_reduce_fusion.places, s32[32]{0:T(128)S(1)} %copy-done.19, s32[8,2]{1,0:T(8,128)S(1)} %copy.35.partners, s32[8]{0:T(128)S(1)} %copy-done.18, ...), custom_call_target="tpu_custom_call", output_to_operand_aliasing={{0}: (13, {})} | custom-call | flops 10485760 | bytes 8192 | tf_op jit(solution)/shard_map/chunk/pallas_call | solution.py:454
  122.3 7.8 %chunk.7 = (bf16[8,16,128,128]{3,2,1,0:T(8,128)(2,1)S(1)}, f32[8,128]{1,0:T(8,128)S(1)}) custom-call(s32[4]{0:T(128)S(1)} %pad_add_fusion.meta, s32[8]{0:T(128)S(1)} %select_reduce_fusion.places, s32[32]{0:T(128)S(1)} %copy-done.19, s32[8,2]{1,0:T(8,128)S(1)} %copy.35.partners, s32[8]{0:T(128)S(1)} %copy-done.18, f32[8,128]{1,0:T(8,128)S(1)} %get-tuple-element.66.after_ref, ...), custom_call_target="tpu_custom_call" | custom-call | flops 4194304 | bytes 8192 | tf_op jit(solution)/shard_map/chunk/pallas_call | solution.py:454
  131.7 3.4 %collective-permute-start.23 = (f32[16,128]{1,0:T(8,128)S(1)}, f32[16,128]{1,0:T(8,128)S(1)}, u32[]{:S(2)}, u32[]{:S(2)}) collective-permute-start(f32[16,128]{1,0:T(8,128)S(1)} %constant_dynamic-update-slice_fusion), channel_id=1, source_target_pairs={{0,12},{4,8},{8,4},{12,0},{1,13},{5,9},{9,5},{13,1},{2,14},{6,10},... | collective-permute-start | bytes 24584 | tf_op jit(solution)/shard_map/ppermute | solution.py:578
  135.4 1.8 %collective-permute-done.23 = f32[16,128]{1,0:T(8,128)S(1)} collective-permute-done((f32[16,128]{1,0:T(8,128)S(1)}, f32[16,128]{1,0:T(8,128)S(1)}, u32[]{:S(2)}, u32[]{:S(2)}) %collective-permute-start.23) | collective-permute-done | bytes 8224 | tf_op jit(solution)/shard_map/ppermute | solution.py:578
  138.3 6.6 %residual.1 = (bf16[8,2,16,128,128]{4,3,2,1,0:T(8,128)(2,1)}, f32[1]{0:T(128)}) custom-call(s32[4]{0:T(128)S(1)} %pad_add_fusion.meta, s32[8]{0:T(128)S(1)} %select_reduce_fusion.places, s32[32]{0:T(128)S(1)} %copy-done.19, s32[8,2]{1,0:T(8,128)S(1)} %copy.35.partners, s32[8]{0:T(128)S(1)} %copy-done.18, f32[16,128]{1,0:T(8,128)S(1)} %add.48.folds_ref, ...), custom_call_target="tpu_custom_call" | custom-call | flops 12582912 | bytes 25165824 | tf_op jit(solution)/shard_map/residual/pallas_call | solution.py:532
  (96 shorter events, 14.4 us)
Async XLA Ops:
  0.6 19.6 %copy-start.19 = (s32[32]{0:T(128)S(1)}, s32[32]{0:T(128)}, u32[]{:S(2)}) copy-start(s32[32]{0:T(128)} %sector_rows.15) | copy-start | bytes 388
  0.6 19.6 %copy-start.18 = (s32[8]{0:T(128)S(1)}, s32[8]{0:T(128)}, u32[]{:S(2)}) copy-start(s32[8]{0:T(128)} %counts.15) | copy-start | bytes 100
  0.7 19.4 %copy-start.20 = (s32[8,2]{0,1:T(2,128)S(1)}, s32[8,2]{0,1:T(2,128)}, u32[]{:S(2)}) copy-start(s32[8,2]{0,1:T(2,128)} %param.14) | copy-start | bytes 196
  6.3 3.3 %collective-permute-start = (bf16[2112,128]{1,0:T(8,128)(2,1)}, bf16[2112,128]{1,0:T(8,128)(2,1)S(1)}, u32[]{:S(2)}, u32[]{:S(2)}) collective-permute-start(bf16[2112,128]{1,0:T(8,128)(2,1)} %get-tuple-element.40), channel_id=1, source_target_pairs={{0,1},{1,0},{2,3},{3,2},{4,5},{5,4},{6,7},{7,6},{8,9},{9,8},{10,11... | collective-permute-start | bytes 1622024 | tf_op jit(solution)/shard_map/ppermute | solution.py:578
  6.8 10.0 %collective-permute-start.2 = (bf16[8,1,128,128]{3,2,1,0:T(8,128)(2,1)}, bf16[8,1,128,128]{3,2,1,0:T(8,128)(2,1)S(1)}, u32[]{:S(2)}, u32[]{:S(2)}) collective-permute-start(bf16[8,1,128,128]{3,2,1,0:T(8,128)(2,1)} %get-tuple-element.44.near_ref), channel_id=1, source_target_pairs={{0,4},{4,0},{8,12},{12,8},{1,5},{5,1},{9,13},{13,9},{2,6},{6,2},{1... | collective-permute-start | bytes 786440 | tf_op jit(solution)/shard_map/ppermute | solution.py:578
  9.4 25.6 %collective-permute-start.4 = (bf16[8,3,128,128]{3,2,1,0:T(8,128)(2,1)}, bf16[8,3,128,128]{3,2,1,0:T(8,128)(2,1)S(1)}, u32[]{:S(2)}, u32[]{:S(2)}) collective-permute-start(bf16[8,3,128,128]{3,2,1,0:T(8,128)(2,1)} %get-tuple-element.50.near_ref), channel_id=1, source_target_pairs={{0,4},{4,0},{8,12},{12,8},{1,5},{5,1},{9,13},{13,9},{2,6},{6,2},{1... | collective-permute-start | bytes 2359304 | tf_op jit(solution)/shard_map/ppermute | solution.py:578
  10.6 40.1 %collective-permute-start.1 = (bf16[2,2112,128]{2,1,0:T(8,128)(2,1)S(1)}, bf16[2,2112,128]{2,1,0:T(8,128)(2,1)S(1)}, u32[]{:S(2)}, u32[]{:S(2)}) collective-permute-start(bf16[2,2112,128]{2,1,0:T(8,128)(2,1)S(1)} %stack.29.rest_0_), channel_id=1, source_target_pairs={{0,2},{1,3},{2,0},{3,1},{4,6},{5,7},{6,4},{7,5},{8,10},{9,11},{10,... | collective-permute-start | bytes 3244040 | tf_op jit(solution)/shard_map/ppermute | solution.py:578
  18.6 16.4 %collective-permute-start.3 = (bf16[2,8,1,128,128]{4,3,2,1,0:T(8,128)(2,1)}, bf16[2,8,1,128,128]{4,3,2,1,0:T(8,128)(2,1)}, u32[]{:S(2)}, u32[]{:S(2)}) collective-permute-start(bf16[2,8,1,128,128]{4,3,2,1,0:T(8,128)(2,1)} %stack.30.rest_2_), channel_id=1, source_target_pairs={{4,8},{8,4},{5,9},{9,5},{6,10},{10,6},{7,11},{11,7},{20,24},{24,20... | collective-permute-start | bytes 1572872 | tf_op jit(solution)/shard_map/ppermute | solution.py:606
  35.0 17.7 %copy-start.5 = (bf16[8,1,8,256,128]{4,3,2,1,0:T(8,128)(2,1)}, bf16[8,1,8,256,128]{4,3,2,1,0:T(8,128)(2,1)S(1)}, u32[]{:S(2)}) copy-start(bf16[8,1,8,256,128]{4,3,2,1,0:T(8,128)(2,1)S(1)} %get-tuple-element.54.rest_0_) | copy-start | bytes 12582916
  35.0 15.8 %collective-permute-start.5 = (bf16[2,8,1,128,128]{4,3,2,1,0:T(8,128)(2,1)}, bf16[2,8,1,128,128]{4,3,2,1,0:T(8,128)(2,1)S(1)}, u32[]{:S(2)}, u32[]{:S(2)}) collective-permute-start(bf16[2,8,1,128,128]{4,3,2,1,0:T(8,128)(2,1)} %collective-permute-done.3.rest_3_), channel_id=1, source_target_pairs={{4,0},{8,12},{5,1},{9,13},{6,2},{10,14},{7,3},{11,15},{20,16},{24,... | collective-permute-start | bytes 1572872 | tf_op jit(solution)/shard_map/ppermute | solution.py:620
  36.3 17.2 %collective-permute-start.9 = (bf16[2,8,1,128,128]{4,3,2,1,0:T(8,128)(2,1)S(1)}, bf16[2,8,1,128,128]{4,3,2,1,0:T(8,128)(2,1)S(1)}, u32[]{:S(2)}, u32[]{:S(2)}) collective-permute-start(bf16[2,8,1,128,128]{4,3,2,1,0:T(8,128)(2,1)S(1)} %stack.33.rest_3_), channel_id=1, source_target_pairs={{4,8},{8,4},{5,9},{9,5},{6,10},{10,6},{7,11},{11,7},{20,24},{24,20... | collective-permute-start | bytes 1572872 | tf_op jit(solution)/shard_map/ppermute | solution.py:606
  52.7 2.1 %collective-permute-start.6 = (bf16[8,1,128,128]{3,2,1,0:T(8,128)(2,1)S(1)}, bf16[8,1,128,128]{3,2,1,0:T(8,128)(2,1)S(1)}, u32[]{:S(2)}, u32[]{:S(2)}) collective-permute-start(bf16[8,1,128,128]{3,2,1,0:T(8,128)(2,1)S(1)} %get-tuple-element.48), channel_id=1, source_target_pairs={{0,1},{1,0},{2,3},{3,2},{4,5},{5,4},{6,7},{7,6},{8,9},{9,8},{10,11... | collective-permute-start | bytes 786440 | tf_op jit(solution)/shard_map/ppermute | solution.py:578
  52.8 11.9 %collective-permute-start.8 = (bf16[2,8,1,128,128]{4,3,2,1,0:T(8,128)(2,1)S(1)}, bf16[2,8,1,128,128]{4,3,2,1,0:T(8,128)(2,1)S(1)}, u32[]{:S(2)}, u32[]{:S(2)}) collective-permute-start(bf16[2,8,1,128,128]{4,3,2,1,0:T(8,128)(2,1)S(1)} %stack.32.rest_3_), channel_id=1, source_target_pairs={{4,8},{8,4},{5,9},{9,5},{6,10},{10,6},{7,11},{11,7},{20,24},{24,20... | collective-permute-start | bytes 1572872 | tf_op jit(solution)/shard_map/ppermute | solution.py:606
  53.5 16.3 %collective-permute-start.10 = (bf16[2,8,1,128,128]{4,3,2,1,0:T(8,128)(2,1)S(1)}, bf16[2,8,1,128,128]{4,3,2,1,0:T(8,128)(2,1)S(1)}, u32[]{:S(2)}, u32[]{:S(2)}) collective-permute-start(bf16[2,8,1,128,128]{4,3,2,1,0:T(8,128)(2,1)S(1)} %collective-permute-done.9.rest_4_), channel_id=1, source_target_pairs={{4,0},{8,12},{5,1},{9,13},{6,2},{10,14},{7,3},{11,15},{20,16},{24,... | collective-permute-start | bytes 1572872 | tf_op jit(solution)/shard_map/ppermute | solution.py:620
  54.9 15.0 %collective-permute-start.7 = (bf16[2,8,1,128,128]{4,3,2,1,0:T(8,128)(2,1)S(1)}, bf16[2,8,1,128,128]{4,3,2,1,0:T(8,128)(2,1)S(1)}, u32[]{:S(2)}, u32[]{:S(2)}) collective-permute-start(bf16[2,8,1,128,128]{4,3,2,1,0:T(8,128)(2,1)S(1)} %stack.31.rest_0_), channel_id=1, source_target_pairs={{0,2},{1,3},{2,0},{3,1},{4,6},{5,7},{6,4},{7,5},{8,10},{9,11},{10,... | collective-permute-start | bytes 1572872 | tf_op jit(solution)/shard_map/ppermute | solution.py:578
  71.1 2.3 %collective-permute-start.11 = (bf16[8,1,128,128]{3,2,1,0:T(8,128)(2,1)S(1)}, bf16[8,1,128,128]{3,2,1,0:T(8,128)(2,1)S(1)}, u32[]{:S(2)}, u32[]{:S(2)}) collective-permute-start(bf16[8,1,128,128]{3,2,1,0:T(8,128)(2,1)S(1)} %get-tuple-element.53), channel_id=1, source_target_pairs={{0,1},{1,0},{2,3},{3,2},{4,5},{5,4},{6,7},{7,6},{8,9},{9,8},{10,11... | collective-permute-start | bytes 786440 | tf_op jit(solution)/shard_map/ppermute | solution.py:578
  71.2 16.4 %collective-permute-start.13 = (bf16[2,8,1,128,128]{4,3,2,1,0:T(8,128)(2,1)S(1)}, bf16[2,8,1,128,128]{4,3,2,1,0:T(8,128)(2,1)S(1)}, u32[]{:S(2)}, u32[]{:S(2)}) collective-permute-start(bf16[2,8,1,128,128]{4,3,2,1,0:T(8,128)(2,1)S(1)} %stack.35.rest_2_), channel_id=1, source_target_pairs={{4,8},{8,4},{5,9},{9,5},{6,10},{10,6},{7,11},{11,7},{20,24},{24,20... | collective-permute-start | bytes 1572872 | tf_op jit(solution)/shard_map/ppermute | solution.py:606
  72.0 17.7 %collective-permute-start.14 = (bf16[2,8,1,128,128]{4,3,2,1,0:T(8,128)(2,1)S(1)}, bf16[2,8,1,128,128]{4,3,2,1,0:T(8,128)(2,1)S(1)}, u32[]{:S(2)}, u32[]{:S(2)}) collective-permute-start(bf16[2,8,1,128,128]{4,3,2,1,0:T(8,128)(2,1)S(1)} %collective-permute-done.8.rest_2_.rest_4_), channel_id=1, source_target_pairs={{4,0},{8,12},{5,1},{9,13},{6,2},{10,14},{7,3},{11,15},{20,16},{24,... | collective-permute-start | bytes 1572872 | tf_op jit(solution)/shard_map/ppermute | solution.py:620
  73.5 16.2 %collective-permute-start.12 = (bf16[2,8,1,128,128]{4,3,2,1,0:T(8,128)(2,1)S(1)}, bf16[2,8,1,128,128]{4,3,2,1,0:T(8,128)(2,1)S(1)}, u32[]{:S(2)}, u32[]{:S(2)}) collective-permute-start(bf16[2,8,1,128,128]{4,3,2,1,0:T(8,128)(2,1)S(1)} %stack.34.after_ref), channel_id=1, source_target_pairs={{0,2},{1,3},{2,0},{3,1},{4,6},{5,7},{6,4},{7,5},{8,10},{9,11},{10,... | collective-permute-start | bytes 1572872 | tf_op jit(solution)/shard_map/ppermute | solution.py:578
  75.0 19.1 %copy-start.2 = (bf16[8,1,8,256,128]{4,3,2,1,0:T(8,128)(2,1)S(1)}, bf16[8,1,8,256,128]{4,3,2,1,0:T(8,128)(2,1)}, u32[]{:S(2)}) copy-start(bf16[8,1,8,256,128]{4,3,2,1,0:T(8,128)(2,1)} %copy-done.1) | copy-start | bytes 12582916
  75.0 19.1 %copy-start.4 = (bf16[8,1,8,256,128]{4,3,2,1,0:T(8,128)(2,1)S(1)}, bf16[8,1,8,256,128]{4,3,2,1,0:T(8,128)(2,1)}, u32[]{:S(2)}) copy-start(bf16[8,1,8,256,128]{4,3,2,1,0:T(8,128)(2,1)} %copy-done.3) | copy-start | bytes 12582916
  91.0 1.6 %collective-permute-start.15 = (bf16[8,1,128,128]{3,2,1,0:T(8,128)(2,1)S(1)}, bf16[8,1,128,128]{3,2,1,0:T(8,128)(2,1)S(1)}, u32[]{:S(2)}, u32[]{:S(2)}) collective-permute-start(bf16[8,1,128,128]{3,2,1,0:T(8,128)(2,1)S(1)} %get-tuple-element.57), channel_id=1, source_target_pairs={{0,1},{1,0},{2,3},{3,2},{4,5},{5,4},{6,7},{7,6},{8,9},{9,8},{10,11... | collective-permute-start | bytes 786440 | tf_op jit(solution)/shard_map/ppermute | solution.py:578
  91.0 16.2 %collective-permute-start.17 = (bf16[2,8,1,128,128]{4,3,2,1,0:T(8,128)(2,1)S(1)}, bf16[2,8,1,128,128]{4,3,2,1,0:T(8,128)(2,1)S(1)}, u32[]{:S(2)}, u32[]{:S(2)}) collective-permute-start(bf16[2,8,1,128,128]{4,3,2,1,0:T(8,128)(2,1)S(1)} %collective-permute-done.13.rest_2_.rest_3_), channel_id=1, source_target_pairs={{4,0},{8,12},{5,1},{9,13},{6,2},{10,14},{7,3},{11,15},{20,16},{24,... | collective-permute-start | bytes 1572872 | tf_op jit(solution)/shard_map/ppermute | solution.py:620
  92.6 14.6 %collective-permute-start.16 = (bf16[2,8,1,128,128]{4,3,2,1,0:T(8,128)(2,1)S(1)}, bf16[2,8,1,128,128]{4,3,2,1,0:T(8,128)(2,1)S(1)}, u32[]{:S(2)}, u32[]{:S(2)}) collective-permute-start(bf16[2,8,1,128,128]{4,3,2,1,0:T(8,128)(2,1)S(1)} %stack.36.after_ref), channel_id=1, source_target_pairs={{0,2},{1,3},{2,0},{3,1},{4,6},{5,7},{6,4},{7,5},{8,10},{9,11},{10,... | collective-permute-start | bytes 1572872 | tf_op jit(solution)/shard_map/ppermute | solution.py:578
  108.7 13.5 %collective-permute-start.19 = (bf16[8,1,128,128]{3,2,1,0:T(8,128)(2,1)S(1)}, bf16[8,1,128,128]{3,2,1,0:T(8,128)(2,1)S(1)}, u32[]{:S(2)}, u32[]{:S(2)}) collective-permute-start(bf16[8,1,128,128]{3,2,1,0:T(8,128)(2,1)S(1)} %get-tuple-element.62.after_ref.rest_4_), channel_id=1, source_target_pairs={{0,2},{1,3},{2,0},{3,1},{4,6},{5,7},{6,4},{7,5},{8,10},{9,11},{10,... | collective-permute-start | bytes 786440 | tf_op jit(solution)/shard_map/ppermute | solution.py:578
  110.2 12.0 %collective-permute-start.20 = (bf16[8,1,128,128]{3,2,1,0:T(8,128)(2,1)S(1)}, bf16[8,1,128,128]{3,2,1,0:T(8,128)(2,1)S(1)}, u32[]{:S(2)}, u32[]{:S(2)}) collective-permute-start(bf16[8,1,128,128]{3,2,1,0:T(8,128)(2,1)S(1)} %get-tuple-element.71), channel_id=1, source_target_pairs={{0,3},{1,2},{2,1},{3,0},{4,7},{5,6},{6,5},{7,4},{8,11},{9,10},{10,... | collective-permute-start | bytes 786440 | tf_op jit(solution)/shard_map/ppermute | solution.py:578
  110.2 12.0 %collective-permute-start.18 = (bf16[8,1,128,128]{3,2,1,0:T(8,128)(2,1)S(1)}, bf16[8,1,128,128]{3,2,1,0:T(8,128)(2,1)S(1)}, u32[]{:S(2)}, u32[]{:S(2)}) collective-permute-start(bf16[8,1,128,128]{3,2,1,0:T(8,128)(2,1)S(1)} %get-tuple-element.71), channel_id=1, source_target_pairs={{0,1},{1,0},{2,3},{3,2},{4,5},{5,4},{6,7},{7,6},{8,9},{9,8},{10,11... | collective-permute-start | bytes 786440 | tf_op jit(solution)/shard_map/ppermute | solution.py:578
  130.1 8.2 %collective-permute-start.25 = (bf16[8,16,128,128]{3,2,1,0:T(8,128)(2,1)S(1)}, bf16[8,16,128,128]{3,2,1,0:T(8,128)(2,1)S(1)}, u32[]{:S(2)}, u32[]{:S(2)}) collective-permute-start(bf16[8,16,128,128]{3,2,1,0:T(8,128)(2,1)S(1)} %get-tuple-element.75.own_ref), channel_id=1, source_target_pairs={{0,1},{1,0},{2,3},{3,2},{4,5},{5,4},{6,7},{7,6},{8,9},{9,8},{10,11... | collective-permute-start | bytes 12582920 | tf_op jit(solution)/shard_map/ppermute | solution.py:578
  130.7 4.4 %collective-permute-start.21 = (f32[16,128]{1,0:T(8,128)S(1)}, f32[16,128]{1,0:T(8,128)S(1)}, u32[]{:S(2)}, u32[]{:S(2)}) collective-permute-start(f32[16,128]{1,0:T(8,128)S(1)} %constant_dynamic-update-slice_fusion), channel_id=1, source_target_pairs={{0,4},{4,0},{8,12},{12,8},{1,5},{5,1},{9,13},{13,9},{2,6},{6,2},{1... | collective-permute-start | bytes 24584 | tf_op jit(solution)/shard_map/ppermute | solution.py:578
  130.8 4.5 %collective-permute-start.22 = (f32[16,128]{1,0:T(8,128)S(1)}, f32[16,128]{1,0:T(8,128)S(1)}, u32[]{:S(2)}, u32[]{:S(2)}) collective-permute-start(f32[16,128]{1,0:T(8,128)S(1)} %constant_dynamic-update-slice_fusion), channel_id=1, source_target_pairs={{0,8},{4,12},{8,0},{12,4},{1,9},{5,13},{9,1},{13,5},{2,10},{6,14},... | collective-permute-start | bytes 24584 | tf_op jit(solution)/shard_map/ppermute | solution.py:578
  131.7 5.4 %collective-permute-start.23 = (f32[16,128]{1,0:T(8,128)S(1)}, f32[16,128]{1,0:T(8,128)S(1)}, u32[]{:S(2)}, u32[]{:S(2)}) collective-permute-start(f32[16,128]{1,0:T(8,128)S(1)} %constant_dynamic-update-slice_fusion), channel_id=1, source_target_pairs={{0,12},{4,8},{8,4},{12,0},{1,13},{5,9},{9,5},{13,1},{2,14},{6,10},... | collective-permute-start | bytes 24584 | tf_op jit(solution)/shard_map/ppermute | solution.py:578
  137.2 1.2 collective-permute-start.24
  (15 other events, 140.9 us)

commit v2 on v1

--- a/solution.py
+++ b/solution.py
@@ -386,9 +386,10 @@
                 ]
                 multiply_left(live_groups, lefts, psi_ref.at[block], after_left)
             targets = [(after_ops, (term,)) for term in range(len(late) * terms)]
-            for group in range(0, live_groups, WIDE):
+            for group in range(0, live_groups, 2 * WIDE):
+                sides = min(2 * WIDE, live_groups - group)
                 if late:
-                    apply_operators(group, group + WIDE, spread_ops, after_left, targets)
+                    apply_operators(group, group + sides, spread_ops, after_left, targets)
                 parts = []
                 for pair in range(0, devices, 2):
                     rows = jnp.concatenate(
@@ -401,7 +402,7 @@
                                 ],
                                 axis=1,
                             )
-                            for side in range(WIDE)
+                            for side in range(sides)
                         ],
                         axis=0,
                     )
@@ -410,8 +411,8 @@
                     )
                 while len(parts) > 1:
                     parts = [parts[at] + parts[at + 1] for at in range(0, len(parts), 2)]
-                done = parts[0].reshape(WIDE, states, TILE, width)
-                for side in range(WIDE):
+                done = parts[0].reshape(sides, states, TILE, width)
+                for side in range(sides):
                     tile = slice((group + side) * TILE, (group + side + 1) * TILE)
                     if first:
                         total[:, tile, :] = done[side]

time: 146 us -> 147 us (level)
  waiting for transfers between devices: 22.3 us -> 33.3 us
  Pallas kernels: 86.5 us -> 76.9 us
    ppermute x4, waiting for transfers between devices: 14.6 us -> 22.4 us  [choose(): pieces = pieces + [lax.ppermute(pieces[-1], 'sec', [(1, 0), (2, 3)])]]
    pallas_call x4, Pallas kernels: 43 us -> 35.8 us  [chunk_call(): pl.pallas_call(functools.partial(chunk_kernel, first, last, held, chunk,...]
    ppermute x18, waiting for transfers between devices: 7.68 us -> 10.9 us  [swap(): return lax.ppermute(value, axis, [(i, i ^ bits) for i in range(size)])]
    pallas_call x3, Pallas kernels: 26.1 us -> 23.7 us  [left_call(): pl.pallas_call(functools.partial(left_kernel, first, held, items, len(pay...]
  transfers between devices with their start and end apart: 26 -> 26, of which waited for: 9 -> 10; matrix products, arithmetic and copies ran while one was open for 0% -> 0% of each run, Pallas kernels for 44% -> 38%
where the time goes in v2:
time: 147 us
  Pallas kernels  76.9 us (52%)
  waiting for transfers between devices  33.3 us (23%)
  starting transfers between devices  26.9 us (18%)
  local copies, waits for them, and re-layouts  7.78 us (5%)
    pallas_call x4, Pallas kernels, chunk_call(): pl.pallas_call(functools.partial(chunk_kernel, first, last, held, chunk,...  35.8 us
    pallas_call x3, Pallas kernels, left_call(): pl.pallas_call(functools.partial(left_kernel, first, held, items, len(pay...  23.7 us
    ppermute x4, waiting for transfers between devices, choose(): pieces = pieces + [lax.ppermute(pieces[-1], 'sec', [(1, 0), (2, 3)])]  22.4 us
    ppermute x18, starting transfers between devices, swap(): return lax.ppermute(value, axis, [(i, i ^ bits) for i in range(size)])  18.1 us
    ppermute x18, waiting for transfers between devices, swap(): return lax.ppermute(value, axis, [(i, i ^ bits) for i in range(size)])  10.9 us
    unnamed x44, local copies, waits for them, and re-layouts  7.12 us
    pallas_call x1, Pallas kernels, residual_call(): pl.pallas_call(functools.partial(residual_kernel, sectors // 2, slots), i...  6.6 us
    pallas_call x4, Pallas kernels, choose_call(): pl.pallas_call(functools.partial(choose_kernel, line, len(pieces), len(af...  5.88 us
  transfers between devices with their start and end apart: 26, of which 10 were waited for; matrix products, arithmetic and copies ran while one was open for 0% of the time, Pallas kernels for 38%

profile of v2, /device:TPU:0, one launch (start us, length us, event | category | flops | bytes accessed | tf_op | source)
XLA Modules:
  0.0 147.4 jit_solution(8267234351069534268)
XLA Ops:
  2.5 3.8 %pack.1 = (bf16[2112,128]{1,0:T(8,128)(2,1)}, bf16[2112,128]{1,0:T(8,128)(2,1)}, bf16[8,1,128,128]{3,2,1,0:T(8,128)(2,1)}, bf16[8,3,128,128]{3,2,1,0:T(8,128)(2,1)}) custom-call(s32[8]{0:T(128)} %dynamic_slice.8.places, s32[4]{0:T(128)} %term_op.1, bf16[8,16,16]{2,1,0:T(8,128)(2,1)} %ops_ref.1, bf16[8,512,128]{2,1,0:T(8,128)(2,1)} %bitcast.5, ...), custom_call_target="tpu_custom_call" | custom-call | bytes 2097152 | tf_op jit(solution)/shard_map/pack/pallas_call | solution.py:145
  6.8 2.6 %collective-permute-start.2 = (bf16[8,1,128,128]{3,2,1,0:T(8,128)(2,1)}, bf16[8,1,128,128]{3,2,1,0:T(8,128)(2,1)S(1)}, u32[]{:S(2)}, u32[]{:S(2)}) collective-permute-start(bf16[8,1,128,128]{3,2,1,0:T(8,128)(2,1)} %get-tuple-element.44.near_ref), channel_id=1, source_target_pairs={{0,4},{4,0},{8,12},{12,8},{1,5},{5,1},{9,13},{13,9},{2,6},{6,2},{1... | collective-permute-start | bytes 786440 | tf_op jit(solution)/shard_map/ppermute | solution.py:579
  10.6 1.9 %collective-permute-start.1 = (bf16[2,2112,128]{2,1,0:T(8,128)(2,1)S(1)}, bf16[2,2112,128]{2,1,0:T(8,128)(2,1)S(1)}, u32[]{:S(2)}, u32[]{:S(2)}) collective-permute-start(bf16[2,2112,128]{2,1,0:T(8,128)(2,1)S(1)} %stack.29.rest_0_), channel_id=1, source_target_pairs={{0,2},{1,3},{2,0},{3,1},{4,6},{5,7},{6,4},{7,5},{8,10},{9,11},{10,... | collective-permute-start | bytes 3244040 | tf_op jit(solution)/shard_map/ppermute | solution.py:579
  12.6 4.2 %collective-permute-done.2.received_ref = bf16[8,1,128,128]{3,2,1,0:T(8,128)(2,1)S(1)} collective-permute-done((bf16[8,1,128,128]{3,2,1,0:T(8,128)(2,1)}, bf16[8,1,128,128]{3,2,1,0:T(8,128)(2,1)S(1)}, u32[]{:S(2)}, u32[]{:S(2)}) %collective-permute-start.2) | collective-permute-done | bytes 262176 | tf_op jit(solution)/shard_map/ppermute | solution.py:579
  18.6 1.5 collective-permute-start.3
  21.2 10.7 %left.3 = (bf16[8,1,8,256,128]{4,3,2,1,0:T(8,128)(2,1)S(1)}, bf16[8,1,8,256,128]{4,3,2,1,0:T(8,128)(2,1)S(1)}, bf16[8,1,8,256,128]{4,3,2,1,0:T(8,128)(2,1)S(1)},...) custom-call(s32[4]{0:T(128)S(1)} %pad_add_fusion.meta, ...), custom_call_target="tpu_custom_call" | custom-call | flops 25165824 | bytes 16384 | tf_op jit(solution)/shard_map/left/pallas_call | solution.py:257
  31.9 2.0 %copy-done.7 = bf16[8,1,8,256,128]{4,3,2,1,0:T(8,128)(2,1)} copy-done((bf16[8,1,8,256,128]{4,3,2,1,0:T(8,128)(2,1)}, bf16[8,1,8,256,128]{4,3,2,1,0:T(8,128)(2,1)S(1)}, u32[]{:S(2)}) %copy-start.7) | copy-done | bytes 4194328
  36.0 7.3 %left.4 = (bf16[8,1,8,256,128]{4,3,2,1,0:T(8,128)(2,1)S(1)}, bf16[8,1,8,256,128]{4,3,2,1,0:T(8,128)(2,1)S(1)}, bf16[8,1,8,256,128]{4,3,2,1,0:T(8,128)(2,1)S(1)}, f32[8,128]{1,0:T(8,128)S(1)}) custom-call(s32[4]{0:T(128)S(1)} %pad_add_fusion.meta, s32[8]{0:T(128)S(1)} %select_reduce_fusion.places, s32[32]{0:T(128)S(1)} %copy-done.19, ...), custom_call_target="tpu_custom_call" | custom-call | flops 9437184 | bytes 8192 | tf_op jit(solution)/shard_map/left/pallas_call | solution.py:257
  43.3 7.6 %collective-permute-done.5.rest_4_ = bf16[2,8,1,128,128]{4,3,2,1,0:T(8,128)(2,1)S(1)} collective-permute-done((bf16[2,8,1,128,128]{4,3,2,1,0:T(8,128)(2,1)}, bf16[2,8,1,128,128]{4,3,2,1,0:T(8,128)(2,1)S(1)}, u32[]{:S(2)}, u32[]{:S(2)}) %collective-permute-start.5) | collective-permute-done | bytes 524320 | tf_op jit(solution)/shard_map/ppermute | solution.py:621
  51.0 1.9 %choose.4 = (bf16[8,1,128,128]{3,2,1,0:T(8,128)(2,1)S(1)}, bf16[8,1,128,128]{3,2,1,0:T(8,128)(2,1)S(1)}) custom-call(s32[4]{0:T(128)S(1)} %pad_add_fusion.meta, s32[8]{0:T(128)S(1)} %select_reduce_fusion.places, s32[8,2]{1,0:T(8,128)S(1)} %copy.35.partners, f32[8,128]{1,0:T(8,128)S(1)} %get-tuple-element.43.rest_0_, ...), custom_call_target="tpu_custom_call" | custom-call | bytes 4096 | tf_op jit(solution)/shard_map/choose/pallas_call | solution.py:328
  55.0 1.6 %collective-permute-start.7 = (bf16[2,8,1,128,128]{4,3,2,1,0:T(8,128)(2,1)S(1)}, bf16[2,8,1,128,128]{4,3,2,1,0:T(8,128)(2,1)S(1)}, u32[]{:S(2)}, u32[]{:S(2)}) collective-permute-start(bf16[2,8,1,128,128]{4,3,2,1,0:T(8,128)(2,1)S(1)} %stack.31.rest_0_), channel_id=1, source_target_pairs={{0,2},{1,3},{2,0},{3,1},{4,6},{5,7},{6,4},{7,5},{8,10},{9,11},{10,... | collective-permute-start | bytes 1572872 | tf_op jit(solution)/shard_map/ppermute | solution.py:579
  56.6 5.7 %left.5 = (bf16[8,1,8,256,128]{4,3,2,1,0:T(8,128)(2,1)S(1)}, bf16[8,1,8,256,128]{4,3,2,1,0:T(8,128)(2,1)S(1)}, f32[8,128]{1,0:T(8,128)S(1)}) custom-call(s32[4]{0:T(128)S(1)} %pad_add_fusion.meta, s32[8]{0:T(128)S(1)} %select_reduce_fusion.places, s32[32]{0:T(128)S(1)} %copy-done.19, s32[8,2]{1,0:T(8,128)S(1)} %copy.35.partners, s32[8]{0:T(128)S(1)} %copy-done.18, ...), custom_call_target="tpu_custom_call" | custom-call | flops 6291456 | bytes 8192 | tf_op jit(solution)/shard_map/left/pallas_call | solution.py:257
  62.3 2.0 %copy-done.11 = bf16[8,1,8,256,128]{4,3,2,1,0:T(8,128)(2,1)} copy-done((bf16[8,1,8,256,128]{4,3,2,1,0:T(8,128)(2,1)}, bf16[8,1,8,256,128]{4,3,2,1,0:T(8,128)(2,1)S(1)}, u32[]{:S(2)}) %copy-start.11) | copy-done | bytes 4194328
  64.3 6.9 %collective-permute-done.10.rest_5_ = bf16[2,8,1,128,128]{4,3,2,1,0:T(8,128)(2,1)S(1)} collective-permute-done((bf16[2,8,1,128,128]{4,3,2,1,0:T(8,128)(2,1)S(1)}, bf16[2,8,1,128,128]{4,3,2,1,0:T(8,128)(2,1)S(1)}, u32[]{:S(2)}, u32[]{:S(2)}) %collective-permute-start.10) | collective-permute-done | bytes 524320 | tf_op jit(solution)/shard_map/ppermute | solution.py:621
  73.3 1.5 collective-permute-start.14
  74.8 1.6 %collective-permute-start.12 = (bf16[2,8,1,128,128]{4,3,2,1,0:T(8,128)(2,1)S(1)}, bf16[2,8,1,128,128]{4,3,2,1,0:T(8,128)(2,1)S(1)}, u32[]{:S(2)}, u32[]{:S(2)}) collective-permute-start(bf16[2,8,1,128,128]{4,3,2,1,0:T(8,128)(2,1)S(1)} %stack.34.after_ref), channel_id=1, source_target_pairs={{0,2},{1,3},{2,0},{3,1},{4,6},{5,7},{6,4},{7,5},{8,10},{9,11},{10,... | collective-permute-start | bytes 1572872 | tf_op jit(solution)/shard_map/ppermute | solution.py:579
  76.4 10.5 %chunk.4 = (f32[8,16,128,128]{3,2,1,0:T(8,128)S(1)}, f32[8,128]{1,0:T(8,128)S(1)}) custom-call(s32[4]{0:T(128)S(1)} %pad_add_fusion.meta, s32[8]{0:T(128)S(1)} %select_reduce_fusion.places, s32[32]{0:T(128)S(1)} %copy-done.19, s32[8,2]{1,0:T(8,128)S(1)} %copy.35.partners, s32[8]{0:T(128)S(1)} %copy-done.18, ...), custom_call_target="tpu_custom_call" | custom-call | flops 13631488 | bytes 8192 | tf_op jit(solution)/shard_map/chunk/pallas_call | solution.py:455
  86.8 4.0 %collective-permute-done.14.rest_5_ = bf16[2,8,1,128,128]{4,3,2,1,0:T(8,128)(2,1)S(1)} collective-permute-done((bf16[2,8,1,128,128]{4,3,2,1,0:T(8,128)(2,1)S(1)}, bf16[2,8,1,128,128]{4,3,2,1,0:T(8,128)(2,1)S(1)}, u32[]{:S(2)}, u32[]{:S(2)}) %collective-permute-start.14) | collective-permute-done | bytes 524320 | tf_op jit(solution)/shard_map/ppermute | solution.py:621
  93.7 1.6 %collective-permute-start.16 = (bf16[2,8,1,128,128]{4,3,2,1,0:T(8,128)(2,1)S(1)}, bf16[2,8,1,128,128]{4,3,2,1,0:T(8,128)(2,1)S(1)}, u32[]{:S(2)}, u32[]{:S(2)}) collective-permute-start(bf16[2,8,1,128,128]{4,3,2,1,0:T(8,128)(2,1)S(1)} %stack.36.after_ref), channel_id=1, source_target_pairs={{0,2},{1,3},{2,0},{3,1},{4,6},{5,7},{6,4},{7,5},{8,10},{9,11},{10,... | collective-permute-start | bytes 1572872 | tf_op jit(solution)/shard_map/ppermute | solution.py:579
  95.3 9.1 %chunk.5 = (f32[8,16,128,128]{3,2,1,0:T(8,128)S(1)}, f32[8,128]{1,0:T(8,128)S(1)}) custom-call(s32[4]{0:T(128)S(1)} %pad_add_fusion.meta, s32[8]{0:T(128)S(1)} %select_reduce_fusion.places, s32[32]{0:T(128)S(1)} %copy-done.19, s32[8,2]{1,0:T(8,128)S(1)} %copy.35.partners, s32[8]{0:T(128)S(1)} %copy-done.18, ...), custom_call_target="tpu_custom_call", output_to_operand_aliasing={{0}: (13, {})} | custom-call | flops 10485760 | bytes 8192 | tf_op jit(solution)/shard_map/chunk/pallas_call | solution.py:455
  104.4 3.9 %collective-permute-done.17.rest_4_ = bf16[2,8,1,128,128]{4,3,2,1,0:T(8,128)(2,1)S(1)} collective-permute-done((bf16[2,8,1,128,128]{4,3,2,1,0:T(8,128)(2,1)S(1)}, bf16[2,8,1,128,128]{4,3,2,1,0:T(8,128)(2,1)S(1)}, u32[]{:S(2)}, u32[]{:S(2)}) %collective-permute-start.17) | collective-permute-done | bytes 524320 | tf_op jit(solution)/shard_map/ppermute | solution.py:621
  108.4 1.5 %choose.7 = (bf16[8,1,128,128]{3,2,1,0:T(8,128)(2,1)S(1)}, bf16[8,1,128,128]{3,2,1,0:T(8,128)(2,1)S(1)}) custom-call(s32[4]{0:T(128)S(1)} %pad_add_fusion.meta, s32[8]{0:T(128)S(1)} %select_reduce_fusion.places, s32[8,2]{1,0:T(8,128)S(1)} %copy.35.partners, f32[8,128]{1,0:T(8,128)S(1)} %get-tuple-element.61.rest_0_, ...), custom_call_target="tpu_custom_call" | custom-call | bytes 4096 | tf_op jit(solution)/shard_map/choose/pallas_call | solution.py:328
  109.9 1.6 %collective-permute-start.19 = (bf16[8,1,128,128]{3,2,1,0:T(8,128)(2,1)S(1)}, bf16[8,1,128,128]{3,2,1,0:T(8,128)(2,1)S(1)}, u32[]{:S(2)}, u32[]{:S(2)}) collective-permute-start(bf16[8,1,128,128]{3,2,1,0:T(8,128)(2,1)S(1)} %get-tuple-element.62.after_ref.rest_4_), channel_id=1, source_target_pairs={{0,2},{1,3},{2,0},{3,1},{4,6},{5,7},{6,4},{7,5},{8,10},{9,11},{10,... | collective-permute-start | bytes 786440 | tf_op jit(solution)/shard_map/ppermute | solution.py:579
  112.1 9.1 %chunk.6 = (f32[8,16,128,128]{3,2,1,0:T(8,128)S(1)}, f32[8,128]{1,0:T(8,128)S(1)}) custom-call(s32[4]{0:T(128)S(1)} %pad_add_fusion.meta, s32[8]{0:T(128)S(1)} %select_reduce_fusion.places, s32[32]{0:T(128)S(1)} %copy-done.19, s32[8,2]{1,0:T(8,128)S(1)} %copy.35.partners, s32[8]{0:T(128)S(1)} %copy-done.18, ...), custom_call_target="tpu_custom_call", output_to_operand_aliasing={{0}: (13, {})} | custom-call | flops 10485760 | bytes 8192 | tf_op jit(solution)/shard_map/chunk/pallas_call | solution.py:455
  122.6 7.1 %chunk.7 = (bf16[8,16,128,128]{3,2,1,0:T(8,128)(2,1)S(1)}, f32[8,128]{1,0:T(8,128)S(1)}) custom-call(s32[4]{0:T(128)S(1)} %pad_add_fusion.meta, s32[8]{0:T(128)S(1)} %select_reduce_fusion.places, s32[32]{0:T(128)S(1)} %copy-done.19, s32[8,2]{1,0:T(8,128)S(1)} %copy.35.partners, s32[8]{0:T(128)S(1)} %copy-done.18, f32[8,128]{1,0:T(8,128)S(1)} %get-tuple-element.66.after_ref, ...), custom_call_target="tpu_custom_call" | custom-call | flops 4194304 | bytes 8192 | tf_op jit(solution)/shard_map/chunk/pallas_call | solution.py:455
  129.7 1.3 collective-permute-start.25
  131.0 1.4 collective-permute-start.21
  132.4 1.6 %collective-permute-start.22 = (f32[16,128]{1,0:T(8,128)S(1)}, f32[16,128]{1,0:T(8,128)S(1)}, u32[]{:S(2)}, u32[]{:S(2)}) collective-permute-start(f32[16,128]{1,0:T(8,128)S(1)} %constant_dynamic-update-slice_fusion), channel_id=1, source_target_pairs={{0,8},{4,12},{8,0},{12,4},{1,9},{5,13},{9,1},{13,5},{2,10},{6,14},... | collective-permute-start | bytes 24584 | tf_op jit(solution)/shard_map/ppermute | solution.py:579
  134.0 1.4 collective-permute-start.23
  135.4 1.5 %collective-permute-done.22 = f32[16,128]{1,0:T(8,128)S(1)} collective-permute-done((f32[16,128]{1,0:T(8,128)S(1)}, f32[16,128]{1,0:T(8,128)S(1)}, u32[]{:S(2)}, u32[]{:S(2)}) %collective-permute-start.22) | collective-permute-done | bytes 8224 | tf_op jit(solution)/shard_map/ppermute | solution.py:579
  137.0 2.5 %collective-permute-done.23 = f32[16,128]{1,0:T(8,128)S(1)} collective-permute-done((f32[16,128]{1,0:T(8,128)S(1)}, f32[16,128]{1,0:T(8,128)S(1)}, u32[]{:S(2)}, u32[]{:S(2)}) %collective-permute-start.23) | collective-permute-done | bytes 8224 | tf_op jit(solution)/shard_map/ppermute | solution.py:579
  140.7 6.6 %residual.1 = (bf16[8,2,16,128,128]{4,3,2,1,0:T(8,128)(2,1)}, f32[1]{0:T(128)}) custom-call(s32[4]{0:T(128)S(1)} %pad_add_fusion.meta, s32[8]{0:T(128)S(1)} %select_reduce_fusion.places, s32[32]{0:T(128)S(1)} %copy-done.19, s32[8,2]{1,0:T(8,128)S(1)} %copy.35.partners, s32[8]{0:T(128)S(1)} %copy-done.18, f32[16,128]{1,0:T(8,128)S(1)} %add.48.folds_ref, ...), custom_call_target="tpu_custom_call" | custom-call | flops 12582912 | bytes 25165824 | tf_op jit(solution)/shard_map/residual/pallas_call | solution.py:533
  (96 shorter events, 18.8 us)
Async XLA Ops:
  0.6 19.6 %copy-start.19 = (s32[32]{0:T(128)S(1)}, s32[32]{0:T(128)}, u32[]{:S(2)}) copy-start(s32[32]{0:T(128)} %sector_rows.15) | copy-start | bytes 388
  0.6 19.6 %copy-start.18 = (s32[8]{0:T(128)S(1)}, s32[8]{0:T(128)}, u32[]{:S(2)}) copy-start(s32[8]{0:T(128)} %counts.15) | copy-start | bytes 100
  0.7 19.4 %copy-start.20 = (s32[8,2]{0,1:T(2,128)S(1)}, s32[8,2]{0,1:T(2,128)}, u32[]{:S(2)}) copy-start(s32[8,2]{0,1:T(2,128)} %param.14) | copy-start | bytes 196
  6.3 3.3 %collective-permute-start = (bf16[2112,128]{1,0:T(8,128)(2,1)}, bf16[2112,128]{1,0:T(8,128)(2,1)S(1)}, u32[]{:S(2)}, u32[]{:S(2)}) collective-permute-start(bf16[2112,128]{1,0:T(8,128)(2,1)} %get-tuple-element.40), channel_id=1, source_target_pairs={{0,1},{1,0},{2,3},{3,2},{4,5},{5,4},{6,7},{7,6},{8,9},{9,8},{10,11... | collective-permute-start | bytes 1622024 | tf_op jit(solution)/shard_map/ppermute | solution.py:579
  6.8 10.0 %collective-permute-start.2 = (bf16[8,1,128,128]{3,2,1,0:T(8,128)(2,1)}, bf16[8,1,128,128]{3,2,1,0:T(8,128)(2,1)S(1)}, u32[]{:S(2)}, u32[]{:S(2)}) collective-permute-start(bf16[8,1,128,128]{3,2,1,0:T(8,128)(2,1)} %get-tuple-element.44.near_ref), channel_id=1, source_target_pairs={{0,4},{4,0},{8,12},{12,8},{1,5},{5,1},{9,13},{13,9},{2,6},{6,2},{1... | collective-permute-start | bytes 786440 | tf_op jit(solution)/shard_map/ppermute | solution.py:579
  9.4 24.5 %collective-permute-start.4 = (bf16[8,3,128,128]{3,2,1,0:T(8,128)(2,1)}, bf16[8,3,128,128]{3,2,1,0:T(8,128)(2,1)S(1)}, u32[]{:S(2)}, u32[]{:S(2)}) collective-permute-start(bf16[8,3,128,128]{3,2,1,0:T(8,128)(2,1)} %get-tuple-element.50.near_ref), channel_id=1, source_target_pairs={{0,4},{4,0},{8,12},{12,8},{1,5},{5,1},{9,13},{13,9},{2,6},{6,2},{1... | collective-permute-start | bytes 2359304 | tf_op jit(solution)/shard_map/ppermute | solution.py:579
  10.6 40.3 %collective-permute-start.1 = (bf16[2,2112,128]{2,1,0:T(8,128)(2,1)S(1)}, bf16[2,2112,128]{2,1,0:T(8,128)(2,1)S(1)}, u32[]{:S(2)}, u32[]{:S(2)}) collective-permute-start(bf16[2,2112,128]{2,1,0:T(8,128)(2,1)S(1)} %stack.29.rest_0_), channel_id=1, source_target_pairs={{0,2},{1,3},{2,0},{3,1},{4,6},{5,7},{6,4},{7,5},{8,10},{9,11},{10,... | collective-permute-start | bytes 3244040 | tf_op jit(solution)/shard_map/ppermute | solution.py:579
  18.6 15.4 %collective-permute-start.3 = (bf16[2,8,1,128,128]{4,3,2,1,0:T(8,128)(2,1)}, bf16[2,8,1,128,128]{4,3,2,1,0:T(8,128)(2,1)}, u32[]{:S(2)}, u32[]{:S(2)}) collective-permute-start(bf16[2,8,1,128,128]{4,3,2,1,0:T(8,128)(2,1)} %stack.30.rest_2_), channel_id=1, source_target_pairs={{4,8},{8,4},{5,9},{9,5},{6,10},{10,6},{7,11},{11,7},{20,24},{24,20... | collective-permute-start | bytes 1572872 | tf_op jit(solution)/shard_map/ppermute | solution.py:607
  33.9 17.0 %collective-permute-start.5 = (bf16[2,8,1,128,128]{4,3,2,1,0:T(8,128)(2,1)}, bf16[2,8,1,128,128]{4,3,2,1,0:T(8,128)(2,1)S(1)}, u32[]{:S(2)}, u32[]{:S(2)}) collective-permute-start(bf16[2,8,1,128,128]{4,3,2,1,0:T(8,128)(2,1)} %collective-permute-done.3.rest_3_), channel_id=1, source_target_pairs={{4,0},{8,12},{5,1},{9,13},{6,2},{10,14},{7,3},{11,15},{20,16},{24,... | collective-permute-start | bytes 1572872 | tf_op jit(solution)/shard_map/ppermute | solution.py:621
  35.3 18.4 %collective-permute-start.9 = (bf16[2,8,1,128,128]{4,3,2,1,0:T(8,128)(2,1)S(1)}, bf16[2,8,1,128,128]{4,3,2,1,0:T(8,128)(2,1)S(1)}, u32[]{:S(2)}, u32[]{:S(2)}) collective-permute-start(bf16[2,8,1,128,128]{4,3,2,1,0:T(8,128)(2,1)S(1)} %stack.33.rest_3_), channel_id=1, source_target_pairs={{4,8},{8,4},{5,9},{9,5},{6,10},{10,6},{7,11},{11,7},{20,24},{24,20... | collective-permute-start | bytes 1572872 | tf_op jit(solution)/shard_map/ppermute | solution.py:607
  43.3 19.0 %copy-start.3 = (bf16[8,1,8,256,128]{4,3,2,1,0:T(8,128)(2,1)}, bf16[8,1,8,256,128]{4,3,2,1,0:T(8,128)(2,1)S(1)}, u32[]{:S(2)}) copy-start(bf16[8,1,8,256,128]{4,3,2,1,0:T(8,128)(2,1)S(1)} %get-tuple-element.59.rest_1_) | copy-start | bytes 12582916
  43.3 19.0 %copy-start.9 = (bf16[8,1,8,256,128]{4,3,2,1,0:T(8,128)(2,1)}, bf16[8,1,8,256,128]{4,3,2,1,0:T(8,128)(2,1)S(1)}, u32[]{:S(2)}) copy-start(bf16[8,1,8,256,128]{4,3,2,1,0:T(8,128)(2,1)S(1)} %get-tuple-element.68.rest_1_) | copy-start | bytes 12582916
  52.8 2.1 %collective-permute-start.6 = (bf16[8,1,128,128]{3,2,1,0:T(8,128)(2,1)S(1)}, bf16[8,1,128,128]{3,2,1,0:T(8,128)(2,1)S(1)}, u32[]{:S(2)}, u32[]{:S(2)}) collective-permute-start(bf16[8,1,128,128]{3,2,1,0:T(8,128)(2,1)S(1)} %get-tuple-element.48), channel_id=1, source_target_pairs={{0,1},{1,0},{2,3},{3,2},{4,5},{5,4},{6,7},{7,6},{8,9},{9,8},{10,11... | collective-permute-start | bytes 786440 | tf_op jit(solution)/shard_map/ppermute | solution.py:579
  53.0 11.3 %collective-permute-start.8 = (bf16[2,8,1,128,128]{4,3,2,1,0:T(8,128)(2,1)S(1)}, bf16[2,8,1,128,128]{4,3,2,1,0:T(8,128)(2,1)S(1)}, u32[]{:S(2)}, u32[]{:S(2)}) collective-permute-start(bf16[2,8,1,128,128]{4,3,2,1,0:T(8,128)(2,1)S(1)} %stack.32.rest_3_), channel_id=1, source_target_pairs={{4,8},{8,4},{5,9},{9,5},{6,10},{10,6},{7,11},{11,7},{20,24},{24,20... | collective-permute-start | bytes 1572872 | tf_op jit(solution)/shard_map/ppermute | solution.py:607
  53.7 17.5 %collective-permute-start.10 = (bf16[2,8,1,128,128]{4,3,2,1,0:T(8,128)(2,1)S(1)}, bf16[2,8,1,128,128]{4,3,2,1,0:T(8,128)(2,1)S(1)}, u32[]{:S(2)}, u32[]{:S(2)}) collective-permute-start(bf16[2,8,1,128,128]{4,3,2,1,0:T(8,128)(2,1)S(1)} %collective-permute-done.9.rest_4_), channel_id=1, source_target_pairs={{4,0},{8,12},{5,1},{9,13},{6,2},{10,14},{7,3},{11,15},{20,16},{24,... | collective-permute-start | bytes 1572872 | tf_op jit(solution)/shard_map/ppermute | solution.py:621
  55.0 16.1 %collective-permute-start.7 = (bf16[2,8,1,128,128]{4,3,2,1,0:T(8,128)(2,1)S(1)}, bf16[2,8,1,128,128]{4,3,2,1,0:T(8,128)(2,1)S(1)}, u32[]{:S(2)}, u32[]{:S(2)}) collective-permute-start(bf16[2,8,1,128,128]{4,3,2,1,0:T(8,128)(2,1)S(1)} %stack.31.rest_0_), channel_id=1, source_target_pairs={{0,2},{1,3},{2,0},{3,1},{4,6},{5,7},{6,4},{7,5},{8,10},{9,11},{10,... | collective-permute-start | bytes 1572872 | tf_op jit(solution)/shard_map/ppermute | solution.py:579
  72.4 2.3 %collective-permute-start.11 = (bf16[8,1,128,128]{3,2,1,0:T(8,128)(2,1)S(1)}, bf16[8,1,128,128]{3,2,1,0:T(8,128)(2,1)S(1)}, u32[]{:S(2)}, u32[]{:S(2)}) collective-permute-start(bf16[8,1,128,128]{3,2,1,0:T(8,128)(2,1)S(1)} %get-tuple-element.53), channel_id=1, source_target_pairs={{0,1},{1,0},{2,3},{3,2},{4,5},{5,4},{6,7},{7,6},{8,9},{9,8},{10,11... | collective-permute-start | bytes 786440 | tf_op jit(solution)/shard_map/ppermute | solution.py:579
  72.6 14.3 %collective-permute-start.13 = (bf16[2,8,1,128,128]{4,3,2,1,0:T(8,128)(2,1)S(1)}, bf16[2,8,1,128,128]{4,3,2,1,0:T(8,128)(2,1)S(1)}, u32[]{:S(2)}, u32[]{:S(2)}) collective-permute-start(bf16[2,8,1,128,128]{4,3,2,1,0:T(8,128)(2,1)S(1)} %stack.35.rest_2_), channel_id=1, source_target_pairs={{4,8},{8,4},{5,9},{9,5},{6,10},{10,6},{7,11},{11,7},{20,24},{24,20... | collective-permute-start | bytes 1572872 | tf_op jit(solution)/shard_map/ppermute | solution.py:607
  73.3 17.6 %collective-permute-start.14 = (bf16[2,8,1,128,128]{4,3,2,1,0:T(8,128)(2,1)S(1)}, bf16[2,8,1,128,128]{4,3,2,1,0:T(8,128)(2,1)S(1)}, u32[]{:S(2)}, u32[]{:S(2)}) collective-permute-start(bf16[2,8,1,128,128]{4,3,2,1,0:T(8,128)(2,1)S(1)} %collective-permute-done.8.rest_2_.rest_4_), channel_id=1, source_target_pairs={{4,0},{8,12},{5,1},{9,13},{6,2},{10,14},{7,3},{11,15},{20,16},{24,... | collective-permute-start | bytes 1572872 | tf_op jit(solution)/shard_map/ppermute | solution.py:621
  74.8 16.0 %collective-permute-start.12 = (bf16[2,8,1,128,128]{4,3,2,1,0:T(8,128)(2,1)S(1)}, bf16[2,8,1,128,128]{4,3,2,1,0:T(8,128)(2,1)S(1)}, u32[]{:S(2)}, u32[]{:S(2)}) collective-permute-start(bf16[2,8,1,128,128]{4,3,2,1,0:T(8,128)(2,1)S(1)} %stack.34.after_ref), channel_id=1, source_target_pairs={{0,2},{1,3},{2,0},{3,1},{4,6},{5,7},{6,4},{7,5},{8,10},{9,11},{10,... | collective-permute-start | bytes 1572872 | tf_op jit(solution)/shard_map/ppermute | solution.py:579
  76.4 18.9 %copy-start.4 = (bf16[8,1,8,256,128]{4,3,2,1,0:T(8,128)(2,1)S(1)}, bf16[8,1,8,256,128]{4,3,2,1,0:T(8,128)(2,1)}, u32[]{:S(2)}) copy-start(bf16[8,1,8,256,128]{4,3,2,1,0:T(8,128)(2,1)} %copy-done.3) | copy-start | bytes 12582916
  92.1 1.6 %collective-permute-start.15 = (bf16[8,1,128,128]{3,2,1,0:T(8,128)(2,1)S(1)}, bf16[8,1,128,128]{3,2,1,0:T(8,128)(2,1)S(1)}, u32[]{:S(2)}, u32[]{:S(2)}) collective-permute-start(bf16[8,1,128,128]{3,2,1,0:T(8,128)(2,1)S(1)} %get-tuple-element.57), channel_id=1, source_target_pairs={{0,1},{1,0},{2,3},{3,2},{4,5},{5,4},{6,7},{7,6},{8,9},{9,8},{10,11... | collective-permute-start | bytes 786440 | tf_op jit(solution)/shard_map/ppermute | solution.py:579
  92.2 16.2 %collective-permute-start.17 = (bf16[2,8,1,128,128]{4,3,2,1,0:T(8,128)(2,1)S(1)}, bf16[2,8,1,128,128]{4,3,2,1,0:T(8,128)(2,1)S(1)}, u32[]{:S(2)}, u32[]{:S(2)}) collective-permute-start(bf16[2,8,1,128,128]{4,3,2,1,0:T(8,128)(2,1)S(1)} %collective-permute-done.13.rest_2_.rest_3_), channel_id=1, source_target_pairs={{4,0},{8,12},{5,1},{9,13},{6,2},{10,14},{7,3},{11,15},{20,16},{24,... | collective-permute-start | bytes 1572872 | tf_op jit(solution)/shard_map/ppermute | solution.py:621
  93.7 14.6 %collective-permute-start.16 = (bf16[2,8,1,128,128]{4,3,2,1,0:T(8,128)(2,1)S(1)}, bf16[2,8,1,128,128]{4,3,2,1,0:T(8,128)(2,1)S(1)}, u32[]{:S(2)}, u32[]{:S(2)}) collective-permute-start(bf16[2,8,1,128,128]{4,3,2,1,0:T(8,128)(2,1)S(1)} %stack.36.after_ref), channel_id=1, source_target_pairs={{0,2},{1,3},{2,0},{3,1},{4,6},{5,7},{6,4},{7,5},{8,10},{9,11},{10,... | collective-permute-start | bytes 1572872 | tf_op jit(solution)/shard_map/ppermute | solution.py:579
  109.9 11.4 %collective-permute-start.19 = (bf16[8,1,128,128]{3,2,1,0:T(8,128)(2,1)S(1)}, bf16[8,1,128,128]{3,2,1,0:T(8,128)(2,1)S(1)}, u32[]{:S(2)}, u32[]{:S(2)}) collective-permute-start(bf16[8,1,128,128]{3,2,1,0:T(8,128)(2,1)S(1)} %get-tuple-element.62.after_ref.rest_4_), channel_id=1, source_target_pairs={{0,2},{1,3},{2,0},{3,1},{4,6},{5,7},{6,4},{7,5},{8,10},{9,11},{10,... | collective-permute-start | bytes 786440 | tf_op jit(solution)/shard_map/ppermute | solution.py:579
  111.4 11.1 %collective-permute-start.20 = (bf16[8,1,128,128]{3,2,1,0:T(8,128)(2,1)S(1)}, bf16[8,1,128,128]{3,2,1,0:T(8,128)(2,1)S(1)}, u32[]{:S(2)}, u32[]{:S(2)}) collective-permute-start(bf16[8,1,128,128]{3,2,1,0:T(8,128)(2,1)S(1)} %get-tuple-element.71), channel_id=1, source_target_pairs={{0,3},{1,2},{2,1},{3,0},{4,7},{5,6},{6,5},{7,4},{8,11},{9,10},{10,... | collective-permute-start | bytes 786440 | tf_op jit(solution)/shard_map/ppermute | solution.py:579
  111.4 11.1 %collective-permute-start.18 = (bf16[8,1,128,128]{3,2,1,0:T(8,128)(2,1)S(1)}, bf16[8,1,128,128]{3,2,1,0:T(8,128)(2,1)S(1)}, u32[]{:S(2)}, u32[]{:S(2)}) collective-permute-start(bf16[8,1,128,128]{3,2,1,0:T(8,128)(2,1)S(1)} %get-tuple-element.71), channel_id=1, source_target_pairs={{0,1},{1,0},{2,3},{3,2},{4,5},{5,4},{6,7},{7,6},{8,9},{9,8},{10,11... | collective-permute-start | bytes 786440 | tf_op jit(solution)/shard_map/ppermute | solution.py:579
  129.7 11.0 %collective-permute-start.25 = (bf16[8,16,128,128]{3,2,1,0:T(8,128)(2,1)S(1)}, bf16[8,16,128,128]{3,2,1,0:T(8,128)(2,1)S(1)}, u32[]{:S(2)}, u32[]{:S(2)}) collective-permute-start(bf16[8,16,128,128]{3,2,1,0:T(8,128)(2,1)S(1)} %get-tuple-element.75.own_ref), channel_id=1, source_target_pairs={{0,1},{1,0},{2,3},{3,2},{4,5},{5,4},{6,7},{7,6},{8,9},{9,8},{10,11... | collective-permute-start | bytes 12582920 | tf_op jit(solution)/shard_map/ppermute | solution.py:579
  131.0 4.5 %collective-permute-start.21 = (f32[16,128]{1,0:T(8,128)S(1)}, f32[16,128]{1,0:T(8,128)S(1)}, u32[]{:S(2)}, u32[]{:S(2)}) collective-permute-start(f32[16,128]{1,0:T(8,128)S(1)} %constant_dynamic-update-slice_fusion), channel_id=1, source_target_pairs={{0,4},{4,0},{8,12},{12,8},{1,5},{5,1},{9,13},{13,9},{2,6},{6,2},{1... | collective-permute-start | bytes 24584 | tf_op jit(solution)/shard_map/ppermute | solution.py:579
  132.4 4.5 %collective-permute-start.22 = (f32[16,128]{1,0:T(8,128)S(1)}, f32[16,128]{1,0:T(8,128)S(1)}, u32[]{:S(2)}, u32[]{:S(2)}) collective-permute-start(f32[16,128]{1,0:T(8,128)S(1)} %constant_dynamic-update-slice_fusion), channel_id=1, source_target_pairs={{0,8},{4,12},{8,0},{12,4},{1,9},{5,13},{9,1},{13,5},{2,10},{6,14},... | collective-permute-start | bytes 24584 | tf_op jit(solution)/shard_map/ppermute | solution.py:579
  134.0 5.4 %collective-permute-start.23 = (f32[16,128]{1,0:T(8,128)S(1)}, f32[16,128]{1,0:T(8,128)S(1)}, u32[]{:S(2)}, u32[]{:S(2)}) collective-permute-start(f32[16,128]{1,0:T(8,128)S(1)} %constant_dynamic-update-slice_fusion), channel_id=1, source_target_pairs={{0,12},{4,8},{8,4},{12,0},{1,13},{5,9},{9,5},{13,1},{2,14},{6,10},... | collective-permute-start | bytes 24584 | tf_op jit(solution)/shard_map/ppermute | solution.py:579
  139.5 1.2 collective-permute-start.24
  (15 other events, 143.7 us)
